TPU v7x, 256 devices: a whole 4x4x8 slice. The times are simulated.
256 devices in a mesh: rep: 64 (over z, x, core), shard: 4 (over y).
Axes of the slice: x: 4, y: 4, z: 8, core: 2. Of those that a mesh axis runs over, the one named last changes fastest.
Arguments:
- inputs: bfloat16 [20480, 4096], P('rep', 'shard'), may hold values from -6 to 6
- weight: float32 [4096, 4096], P('shard', 'rep'), may hold values from -0.09375 to 0.09375
- table: bfloat16 [256, 4096], replicated, may hold values from -6 to 6
- targets: int32 [20480], P(('rep', 'shard')), may hold values from 0 to 255
Outputs:
- combined: float32 [4096, 4096], P('shard', 'rep')
- new_weight: float32 [4096, 4096], P('shard', 'rep')
All inputs are finite; a program needn't handle non-finite values.
Results may differ from a plain program's by a relative error of at most 0.005.
Values may be sent and summed in bfloat16 or wider, within the bound.
A program may use at most 128 MiB of HBM per device.

v0:
```python
import functools

import jax
import jax.numpy as jnp
from jax import lax
from jax.sharding import Mesh
from jax.sharding import PartitionSpec as P

REP_SHARD = ("rep_0", "rep_1", "rep_2", "shard")
REP = ("rep_0", "rep_1", "rep_2")


epsilon = 1e-06
step_size = 0.05


def over_axes(shard, axes):
    return functools.reduce(lax.psum, axes, shard)


def joined_along(parts, dim):
    lengths = list(parts.shape[1:])
    lengths[dim] *= parts.shape[0]
    return jnp.moveaxis(parts, 0, dim).reshape(lengths)


def from_everyone(shard, axis):
    peers = lax.axis_size(axis)
    return lax.all_to_all(
        jnp.broadcast_to(shard[None], (peers, *shard.shape)), axis, 0, 0, tiled=True
    )


def gather_directly(shard, axis, dim):
    return joined_along(from_everyone(shard, axis), dim)


def from_partner(block, axis, bit):
    count = lax.axis_size(axis)
    route = []
    for low in range(count):
        high = low | 1 << bit
        if high != low and high < count:
            route += [(low, high), (high, low)]
    return lax.ppermute(block, axis, route)


def adasum_mix(lower_vec, upper_vec, cross, norm_low, norm_high):
    return (1.0 - cross / (2.0 * (norm_low + epsilon))) * lower_vec + (
        1.0 - cross / (2.0 * (norm_high + epsilon))
    ) * upper_vec


def group_sums(partials, depth_bit, my_index, replica_count):
    group_count = replica_count >> depth_bit + 1
    slot = my_index >> depth_bit + 1
    one_hot = (jnp.arange(group_count, dtype=jnp.int32) == slot).astype(jnp.float32)
    tables = (
        over_axes(one_hot * partials[0], REP_SHARD),
        over_axes(one_hot * partials[1], REP_SHARD),
        over_axes(one_hot * partials[2], REP_SHARD),
    )
    return tuple((jnp.sum(entry * one_hot) for entry in tables))


def on_device(inputs, weight, table, targets):
    replica_count = lax.axis_size(REP)
    row_count = inputs.shape[0]
    feature_rows = weight.shape[0]
    block_cols = weight.shape[1]
    weight_full = lax.all_gather(weight.astype(jnp.bfloat16), REP, axis=1, tiled=True)
    row_block = inputs
    outputs = lax.psum_scatter(
        jnp.dot(row_block, weight_full, preferred_element_type=jnp.float32),
        "shard",
        scatter_dimension=0,
        tiled=True,
    )
    wanted = table[targets].astype(jnp.float32)
    error = ((outputs - wanted) / row_count).astype(jnp.bfloat16)
    row_block = inputs
    grad = lax.dot_general(
        row_block,
        gather_directly(error, "shard", 0),
        (((0,), (0,)), ((), ())),
        preferred_element_type=jnp.float32,
    )
    level_count = replica_count.bit_length() - 1
    my_index = lax.axis_index(REP)
    current = grad.reshape(feature_rows, replica_count, block_cols)
    for depth_bit in range(level_count):
        halves = current.reshape(feature_rows, current.shape[1] // 2, 2, block_cols)
        own_bit = my_index >> depth_bit & 1
        kept = jnp.where(own_bit == 1, halves[:, :, 1], halves[:, :, 0])
        outgoing = jnp.where(own_bit == 1, halves[:, :, 0], halves[:, :, 1])
        incoming = from_partner(outgoing, REP, depth_bit)
        lower_vec = jnp.where(own_bit == 1, incoming, kept)
        upper_vec = jnp.where(own_bit == 1, kept, incoming)
        partials = (
            jnp.sum(lower_vec * upper_vec),
            jnp.sum(lower_vec * lower_vec),
            jnp.sum(upper_vec * upper_vec),
        )
        cross, norm_low, norm_high = group_sums(partials, depth_bit, my_index, replica_count)
        current = adasum_mix(lower_vec, upper_vec, cross, norm_low, norm_high)
    combined = current.reshape(feature_rows, block_cols)
    return (combined, weight - step_size * combined)


def solution(mesh):
    split = Mesh(
        mesh.devices.reshape(8, 4, 2, mesh.shape["shard"]), ("rep_0", "rep_1", "rep_2", "shard")
    )
    return jax.shard_map(
        on_device,
        mesh=split,
        in_specs=(P(REP, "shard"), P("shard", REP), P(), P(REP_SHARD)),
        out_specs=(P("shard", REP), P("shard", REP)),
        check_vma=False,
    )
```

profile of v0, /device:TPU:1, one launch (start us, length us, event | category | flops | bytes accessed | tf_op | source)
XLA Modules:
  0.0 769.1 jit_solution(6782132581145719275)
XLA Ops:
  9.1 89.5 %all-gather.2.cloned.1.call-done = bf16[1024,4096]{0,1:T(8,128)(2,1)} async-done(((bf16[1024,64]{0,1:T(8,128)(2,1)}), bf16[1024,4096]{0,1:T(8,128)(2,1)}) %all-gather.2.cloned.1.call-update) | async-done | bytes 8388624 | tf_op jit(solution)/shard_map/all_gather | solution.py:71
  98.6 8.9 %fusion.20 = f32[320,4096]{1,0:T(8,128)} fusion(bf16[320,1024]{1,0:T(8,128)(2,1)} %param.4, bf16[1024,4096]{0,1:T(8,128)(2,1)} %all-gather.2.cloned.1.call-done), kind=kOutput, calls=%fused_computation.94 | convolution fusion | flops 2684354560 | bytes 14286848 | tf_op jit(solution)/shard_map/dot_general | solution.py:74
  109.1 53.4 %reduce-scatter.2.cloned.1.call-done = f32[80,4096]{1,0:T(8,128)} async-done(((f32[320,4096]{1,0:T(8,128)}), f32[80,4096]{1,0:T(8,128)}) %reduce-scatter.2.cloned.1.call-update) | async-done | bytes 1310736 | tf_op jit(solution)/shard_map/reduce_scatter | solution.py:73
  170.4 31.4 %all-to-all-done = bf16[4,80,4096]{2,1,0:T(8,128)(2,1)} async-done(((bf16[4,80,4096]{2,1,0:T(8,128)(2,1)}), bf16[4,80,4096]{2,1,0:T(8,128)(2,1)}, u32[]{:S(2)}, u32[]{:S(2)}) %all-to-all-start) | async-done | bytes 2621472 | tf_op jit(solution)/shard_map/all_to_all | solution.py:29
  201.9 9.9 %fusion.21 = f32[4096,1024]{1,0:T(8,128)} fusion(bf16[320,4096]{1,0:T(8,128)(2,1)} %bitcast.1, bf16[320,1024]{1,0:T(8,128)(2,1)S(1)} %copy-done.4), kind=kOutput, calls=%fused_computation.95 | convolution fusion | flops 2684354560 | bytes 20054016 | tf_op jit(solution)/shard_map/dot_general | solution.py:82
  211.8 12.0 %select_bitcast_fusion = f32[1024,32,64]{0,2,1:T(8,128)} fusion(f32[1024,32,2,64]{0,3,2,1:T(8,128)} %bitcast.153, pred[]{:T(512)S(6)} %eq.90), kind=kLoop, calls=%fused_computation.9 | loop fusion | flops 2097152 | bytes 25165824 | tf_op jit(solution)/shard_map/jit(_where)/select_n | solution.py:95
  225.3 13.1 %collective-permute-done = f32[1024,32,64]{0,2,1:T(8,128)} collective-permute-done((f32[1024,32,64]{0,2,1:T(8,128)}, f32[1024,32,64]{0,2,1:T(8,128)}, u32[]{:S(2)}, u32[]{:S(2)}) %collective-permute-start) | collective-permute-done | bytes 8388640 | tf_op jit(solution)/shard_map/ppermute | solution.py:45
  238.4 14.7 %multiply_reduce_fusion.1 = (f32[]{:T(128)}, f32[]{:T(128)}, f32[]{:T(128)}, f32[1024,32,64]{0,2,1:T(8,128)}, f32[1024,32,64]{0,2,1:T(8,128)}) fusion(f32[1024,32,64]{0,2,1:T(8,128)} %collective-permute-done, f32[1024,32,2,64]{0,3,2,1:T(8,128)} %bitcast.154, pred[]{:T(512)S(6)} %eq.90), kind=kLoop, calls=%fused_computation.7 | loop fusion | flops 18874364 | bytes 41944076 | tf_op jit(solution)/shard_map/reduce_sum | solution.py:101
  254.9 14.0 %all-reduce.5 = (f32[32]{0:T(128)S(1)}, f32[32]{0:T(128)S(1)}, f32[32]{0:T(128)S(1)}) all-reduce(f32[32]{0:T(128)S(1)} %fusion.7, f32[32]{0:T(128)S(1)} %get-tuple-element.106, f32[32]{0:T(128)S(1)} %get-tuple-element.107), channel_id=1, replica_groups=mesh['rep_0'=8,'rep_1'=4,'rep_2'=2,'shard'=4] {'rep_0'}, use_global_device_ids=true, to_apply=%region_2.3 | all-reduce | flops 96 | bytes 768 | tf_op jit(solution)/shard_map/psum | solution.py:18
  296.9 12.1 %multiply_add_fusion = f32[1024,32,64]{0,2,1:T(8,128)} fusion(f32[1024,32,64]{0,2,1:T(8,128)} %get-tuple-element.105, f32[1024,32,64]{0,2,1:T(8,128)} %get-tuple-element.104, f32[]{:T(128)S(6)} %sub.50, f32[]{:T(128)S(6)} %sub.49), kind=kLoop, calls=%fused_computation.5 | loop fusion | flops 6291456 | bytes 25165832 | tf_op jit(solution)/shard_map/add | solution.py:49
  315.7 90.0 %collective-permute-done.1 = f32[1024,16,64]{0,2,1:T(8,128)} collective-permute-done((f32[1024,16,64]{0,2,1:T(8,128)}, f32[1024,16,64]{0,2,1:T(8,128)}, u32[]{:S(2)}, u32[]{:S(2)}) %collective-permute-start.1) | collective-permute-done | bytes 4194336 | tf_op jit(solution)/shard_map/ppermute | solution.py:45
  416.3 11.5 %all-reduce.4 = (f32[16]{0:T(128)S(1)}, f32[16]{0:T(128)S(1)}, f32[16]{0:T(128)S(1)}) all-reduce(f32[16]{0:T(128)S(1)} %fusion.10, f32[16]{0:T(128)S(1)} %fusion.8, f32[16]{0:T(128)S(1)} %fusion.9), channel_id=1, replica_groups=mesh['rep_0'=8,'rep_1'=4,'rep_2'=2,'shard'=4] {'rep_0'}, use_global_device_ids=true, to_apply=%region_20.21 | all-reduce | flops 48 | bytes 384 | tf_op jit(solution)/shard_map/psum | solution.py:18
  433.8 10.9 %all-reduce.22 = (f32[16]{0:T(128)S(1)}, f32[16]{0:T(128)S(1)}, f32[16]{0:T(128)S(1)}) all-reduce(f32[16]{0:T(128)S(1)} %get-tuple-element.68, f32[16]{0:T(128)S(1)} %get-tuple-element.69, f32[16]{0:T(128)S(1)} %get-tuple-element.70), channel_id=1, replica_groups=mesh['rep_0'=8,'rep_1'=4,'rep_2'=2,'shard'=4] {'rep_2'}, use_global_device_ids=true, to_apply=%region_22.23 | all-reduce | flops 48 | bytes 384 | tf_op jit(solution)/shard_map/psum | solution.py:18
  463.1 45.8 %collective-permute-done.2 = f32[1024,8,64]{0,2,1:T(8,128)} collective-permute-done((f32[1024,8,64]{0,2,1:T(8,128)S(1)}, f32[1024,8,64]{0,2,1:T(8,128)}, u32[]{:S(2)}, u32[]{:S(2)}) %collective-permute-start.2) | collective-permute-done | bytes 2097184 | tf_op jit(solution)/shard_map/ppermute | solution.py:45
  517.7 11.8 %all-reduce.3 = (f32[8]{0:T(128)S(1)}, f32[8]{0:T(128)S(1)}, f32[8]{0:T(128)S(1)}) all-reduce(f32[8]{0:T(128)S(1)} %fusion.13, f32[8]{0:T(128)S(1)} %fusion.11, f32[8]{0:T(128)S(1)} %fusion.12), channel_id=1, replica_groups=mesh['rep_0'=8,'rep_1'=4,'rep_2'=2,'shard'=4] {'rep_0'}, use_global_device_ids=true, to_apply=%region_38.39 | all-reduce | flops 24 | bytes 192 | tf_op jit(solution)/shard_map/psum | solution.py:18
  536.9 10.9 %all-reduce.21 = (f32[8]{0:T(128)S(1)}, f32[8]{0:T(128)S(1)}, f32[8]{0:T(128)S(1)}) all-reduce(f32[8]{0:T(128)S(1)} %get-tuple-element.65, f32[8]{0:T(128)S(1)} %get-tuple-element.66, f32[8]{0:T(128)S(1)} %get-tuple-element.67), channel_id=1, replica_groups=mesh['rep_0'=8,'rep_1'=4,'rep_2'=2,'shard'=4] {'rep_2'}, use_global_device_ids=true, to_apply=%region_40.41 | all-reduce | flops 24 | bytes 192 | tf_op jit(solution)/shard_map/psum | solution.py:18
  563.8 21.9 %collective-permute-done.3 = f32[1024,4,64]{0,2,1:T(8,128)S(1)} collective-permute-done((f32[1024,4,64]{0,2,1:T(8,128)}, f32[1024,4,64]{0,2,1:T(8,128)S(1)}, u32[]{:S(2)}, u32[]{:S(2)}) %collective-permute-start.3) | collective-permute-done | bytes 1048608 | tf_op jit(solution)/shard_map/ppermute | solution.py:45
  590.0 11.5 %all-reduce.2 = (f32[4]{0:T(128)S(1)}, f32[4]{0:T(128)S(1)}, f32[4]{0:T(128)S(1)}) all-reduce(f32[4]{0:T(128)S(1)} %fusion.16, f32[4]{0:T(128)S(1)} %fusion.14, f32[4]{0:T(128)S(1)} %fusion.15), channel_id=1, replica_groups=mesh['rep_0'=8,'rep_1'=4,'rep_2'=2,'shard'=4] {'rep_0'}, use_global_device_ids=true, to_apply=%region_56.57 | all-reduce | flops 12 | bytes 96 | tf_op jit(solution)/shard_map/psum | solution.py:18
  607.5 10.9 %all-reduce.20 = (f32[4]{0:T(128)S(1)}, f32[4]{0:T(128)S(1)}, f32[4]{0:T(128)S(1)}) all-reduce(f32[4]{0:T(128)S(1)} %get-tuple-element.62, f32[4]{0:T(128)S(1)} %get-tuple-element.63, f32[4]{0:T(128)S(1)} %get-tuple-element.64), channel_id=1, replica_groups=mesh['rep_0'=8,'rep_1'=4,'rep_2'=2,'shard'=4] {'rep_2'}, use_global_device_ids=true, to_apply=%region_58.59 | all-reduce | flops 12 | bytes 96 | tf_op jit(solution)/shard_map/psum | solution.py:18
  632.0 25.7 %collective-permute-done.4 = f32[1024,2,64]{0,2,1:T(8,128)} collective-permute-done((f32[1024,2,64]{0,2,1:T(8,128)}, f32[1024,2,64]{0,2,1:T(8,128)}, u32[]{:S(2)}, u32[]{:S(2)}) %collective-permute-start.4) | collective-permute-done | bytes 524320 | tf_op jit(solution)/shard_map/ppermute | solution.py:45
  662.4 11.7 %all-reduce.1 = (f32[2]{0:T(128)S(1)}, f32[2]{0:T(128)S(1)}, f32[2]{0:T(128)S(1)}) all-reduce(f32[2]{0:T(128)S(1)} %fusion.19, f32[2]{0:T(128)S(1)} %fusion.17, f32[2]{0:T(128)S(1)} %fusion.18), channel_id=1, replica_groups=mesh['rep_0'=8,'rep_1'=4,'rep_2'=2,'shard'=4] {'rep_0'}, use_global_device_ids=true, to_apply=%region_74.75 | all-reduce | flops 6 | bytes 48 | tf_op jit(solution)/shard_map/psum | solution.py:18
  705.5 14.9 %collective-permute-done.5 = f32[1024,1,64]{0,2,1:T(8,128)} collective-permute-done((f32[1024,1,64]{0,2,1:T(8,128)S(1)}, f32[1024,1,64]{0,2,1:T(8,128)}, u32[]{:S(2)}, u32[]{:S(2)}) %collective-permute-start.5) | collective-permute-done | bytes 262176 | tf_op jit(solution)/shard_map/ppermute | solution.py:45
  724.0 11.4 %all-reduce = (f32[1]{0:T(128)}, f32[1]{0:T(128)}, f32[1]{0:T(128)}) all-reduce(f32[1]{0:T(128)S(6)} %mul.432, f32[1]{0:T(128)S(6)} %mul.443, f32[1]{0:T(128)S(6)} %mul.436), channel_id=1, replica_groups=mesh['rep_0'=8,'rep_1'=4,'rep_2'=2,'shard'=4] {'rep_0'}, use_global_device_ids=true, to_apply=%region_92.93 | all-reduce | flops 3 | bytes 24 | tf_op jit(solution)/shard_map/psum | solution.py:18
  742.1 10.0 %all-reduce.18 = (f32[1]{0:T(128)}, f32[1]{0:T(128)}, f32[1]{0:T(128)}) all-reduce(f32[1]{0:T(128)} %get-tuple-element.56, f32[1]{0:T(128)} %get-tuple-element.57, f32[1]{0:T(128)} %get-tuple-element.58), channel_id=1, replica_groups=mesh['rep_0'=8,'rep_1'=4,'rep_2'=2,'shard'=4] {'rep_2'}, use_global_device_ids=true, to_apply=%region_94.95 | all-reduce | flops 3 | bytes 24 | tf_op jit(solution)/shard_map/psum | solution.py:18
  (87 shorter events, 179.7 us)
Async XLA Ops:
  7.2 101.0 %copy-start = (bf16[256,4096]{1,0:T(8,128)(2,1)S(1)}, bf16[256,4096]{1,0:T(8,128)(2,1)}, u32[]{:S(2)}) copy-start(bf16[256,4096]{1,0:T(8,128)(2,1)} %param.6) | copy-start | bytes 6291460
  7.2 91.4 %all-gather.2.cloned.1.call-start = ((), (), s32[]{:S(2)}) async-start(), calls=%async_computation.2 | async-start | bytes 8519680 | tf_op jit(solution)/shard_map/all_gather | solution.py:71
  9.0 153.5 %reduce-scatter.2.cloned.1.call-start = ((), (), s32[]{:S(2)}) async-start(), calls=%async_computation.3 | async-start | bytes 6553600 | tf_op jit(solution)/shard_map/reduce_scatter | solution.py:73
  107.5 0.7 copy-start.5
  164.0 37.8 %copy-start.4 = (bf16[320,1024]{1,0:T(8,128)(2,1)S(1)}, bf16[320,1024]{1,0:T(8,128)(2,1)}, u32[]{:S(2)}) copy-start(bf16[320,1024]{1,0:T(8,128)(2,1)} %param.4) | copy-start | bytes 1966084
  165.8 36.0 %all-to-all-start = ((bf16[4,80,4096]{2,1,0:T(8,128)(2,1)}), bf16[4,80,4096]{2,1,0:T(8,128)(2,1)}, u32[]{:S(2)}, u32[]{:S(2)}) async-start(bf16[4,80,4096]{2,1,0:T(8,128)(2,1)} %broadcast_in_dim.10), calls=%async_computation.1 | async-start | bytes 5242880 | tf_op jit(solution)/shard_map/all_to_all | solution.py:29
  223.8 14.6 %collective-permute-start = (f32[1024,32,64]{0,2,1:T(8,128)}, f32[1024,32,64]{0,2,1:T(8,128)}, u32[]{:S(2)}, u32[]{:S(2)}) collective-permute-start(f32[1024,32,64]{0,2,1:T(8,128)} %select_bitcast_fusion), channel_id=1, source_target_pairs={{0,4},{4,0},{8,12},{12,8},{16,20},{20,16},{24,28},{28,24},{32,36},... | collective-permute-start | bytes 25165832 | tf_op jit(solution)/shard_map/ppermute | solution.py:45
  315.7 90.0 %collective-permute-start.1 = (f32[1024,16,64]{0,2,1:T(8,128)}, f32[1024,16,64]{0,2,1:T(8,128)}, u32[]{:S(2)}, u32[]{:S(2)}) collective-permute-start(f32[1024,16,64]{0,2,1:T(8,128)} %fusion.1), channel_id=1, source_target_pairs={{0,8},{8,0},{4,12},{12,4},{16,24},{24,16},{20,28},{28,20},{32,40},... | collective-permute-start | bytes 12582920 | tf_op jit(solution)/shard_map/ppermute | solution.py:45
  460.1 1.9 copy-start.2
  462.5 46.5 %collective-permute-start.2 = (f32[1024,8,64]{0,2,1:T(8,128)S(1)}, f32[1024,8,64]{0,2,1:T(8,128)}, u32[]{:S(2)}, u32[]{:S(2)}) collective-permute-start(f32[1024,8,64]{0,2,1:T(8,128)S(1)} %fusion.2), channel_id=1, source_target_pairs={{0,16},{16,0},{4,20},{20,4},{8,24},{24,8},{12,28},{28,12},{32,48},... | collective-permute-start | bytes 6291464 | tf_op jit(solution)/shard_map/ppermute | solution.py:45
  563.2 22.5 %collective-permute-start.3 = (f32[1024,4,64]{0,2,1:T(8,128)}, f32[1024,4,64]{0,2,1:T(8,128)S(1)}, u32[]{:S(2)}, u32[]{:S(2)}) collective-permute-start(f32[1024,4,64]{0,2,1:T(8,128)} %fusion.3), channel_id=1, source_target_pairs={{0,32},{32,0},{4,36},{36,4},{8,40},{40,8},{12,44},{44,12},{16,48},... | collective-permute-start | bytes 3145736 | tf_op jit(solution)/shard_map/ppermute | solution.py:45
  631.1 130.3 %copy-start.3 = (f32[1024,64]{0,1:T(8,128)S(1)}, f32[1024,64]{0,1:T(8,128)}, u32[]{:S(2)}) copy-start(f32[1024,64]{0,1:T(8,128)} %param.5) | copy-start | bytes 786436
  631.1 131.1 %copy-start.1 = (bf16[256,4096]{1,0:T(8,128)(2,1)S(1)}, bf16[256,4096]{1,0:T(8,128)(2,1)}, u32[]{:S(2)}) copy-start(bf16[256,4096]{1,0:T(8,128)(2,1)} %param.6) | copy-start | bytes 6291460
  632.0 25.7 %collective-permute-start.4 = (f32[1024,2,64]{0,2,1:T(8,128)}, f32[1024,2,64]{0,2,1:T(8,128)}, u32[]{:S(2)}, u32[]{:S(2)}) collective-permute-start(f32[1024,2,64]{0,2,1:T(8,128)} %fusion.4), channel_id=1, source_target_pairs={{0,64},{64,0},{4,68},{68,4},{8,72},{72,8},{12,76},{76,12},{16,80},... | collective-permute-start | bytes 1572872 | tf_op jit(solution)/shard_map/ppermute | solution.py:45
  703.0 17.4 %collective-permute-start.5 = (f32[1024,1,64]{0,2,1:T(8,128)S(1)}, f32[1024,1,64]{0,2,1:T(8,128)}, u32[]{:S(2)}, u32[]{:S(2)}) collective-permute-start(f32[1024,1,64]{0,2,1:T(8,128)S(1)} %select_bitcast_fusion.1), channel_id=1, source_target_pairs={{0,128},{128,0},{4,132},{132,4},{8,136},{136,8},{12,140},{140,12},... | collective-permute-start | bytes 786440 | tf_op jit(solution)/shard_map/ppermute | solution.py:45
Sparse Core Ops, SparseCore 0:
  11.4 87.1 all-gather.1
  107.6 54.8 reduce-scatter.1
where the time goes:
time: 771 us; the launch traced here: 769 us
  waiting for transfers between devices  386 us (50%)
  blocking collectives  215 us (28%)
  other arithmetic  103 us (13%)
  between operations  31.4 us (4%)
  matrix products  18.8 us (2%)
  starting transfers between devices  9.92 us (1%)
    psum x24, blocking collectives, over_axes(): return functools.reduce(lax.psum, axes, shard)  215 us
    ppermute x6, waiting for transfers between devices, from_partner(): return lax.ppermute(block, axis, route)  211 us
    all_gather x1, waiting for transfers between devices, on_device(): lax.all_gather(weight.astype(jnp.bfloat16), REP, axis=1, tiled=True)  89.5 us
    reduce_scatter x1, waiting for transfers between devices, on_device(): lax.psum_scatter(jnp.dot(row_block, weight_full, preferred_element_type=j...  53.4 us
    reduce_sum x6, other arithmetic, on_device(): jnp.sum(lower_vec * lower_vec)  36.9 us
    all_to_all x1, waiting for transfers between devices, from_everyone(): lax.all_to_all(jnp.broadcast_to(shard[None], (peers, *shard.shape)), axis...  31.4 us
    select_n x6, other arithmetic, on_device(): outgoing = jnp.where(own_bit == 1, halves[:, :, 0], halves[:, :, 1])  21.3 us
    add x4, other arithmetic, adasum_mix(): (1.0 - cross / (2.0 * (norm_low + epsilon))) * lower_vec  21.1 us
  transfers between devices with their start and end apart: 9, of which 9 were waited for; matrix products, arithmetic and copies ran while one was open for 0% of the time, Pallas kernels for 0%

commit v1 on v0

v1 whole, which is shorter than its diff:
```python
import functools

import jax
import jax.numpy as jnp
from jax import lax
from jax.experimental import pallas as pl
from jax.experimental.pallas import tpu as pltpu
from jax.sharding import Mesh
from jax.sharding import PartitionSpec as P

AXES = ("z", "x", "c", "shard")
REP = ("z", "x", "c")
MESH = pl.DeviceIdType.MESH
F32, BF16 = jnp.float32, jnp.bfloat16

EPS = 1e-06
STEP = 0.05

KX = (0, 0, -1, 1, -1, 1, 2, 2)
KC = (0, 1, 0, 0, 1, 1, 0, 1)
DZ = (0, -1, 1, -2, 2, -3, 3, 4)

ROWS, FEAT, PIECE, HALF = 320, 1024, 80, 256
UNITS = 16


def place_of(steps, other):
    return [i for i in range(8) if KX[i] % 4 == steps % 4 and KC[i] == other][0]


def block_of(steps):
    return [i for i in range(8) if DZ[i] % 8 == steps % 8][0]


def iotas(shape):
    return lax.broadcasted_iota(jnp.int32, shape, 0), lax.broadcasted_iota(jnp.int32, shape, 1)


def swap_bit(v, bit, axis):
    pos = lax.broadcasted_iota(jnp.int32, v.shape, axis)
    up = pltpu.roll(v, bit, axis)
    down = pltpu.roll(v, v.shape[axis] - bit, axis)
    return jnp.where((pos & bit) != 0, up, down)


def tree_coefficients(gram):
    sub, lane = iotas(gram.shape)
    coef = jnp.ones((8, 1), F32)
    for bit in (1, 2, 4):
        own = jnp.where(lane == sub, gram, 0.0)
        cross = jnp.where(lane == (sub ^ bit), gram, 0.0)

        def factor(axis):
            norm = jnp.maximum(jnp.sum(own, axis=axis, keepdims=True), 0.0)
            return 1.0 - jnp.sum(cross, axis=axis, keepdims=True) / (2.0 * (norm + EPS))

        by_row, by_col = factor(1), factor(0)
        coef = coef * by_row
        gram = gram * by_row * by_col
        gram = gram + swap_bit(gram, bit, 1)
        gram = gram + swap_bit(gram, bit, 0)
    return coef


def pick(coef, index):
    sub, _ = iotas((8, 1))
    return jnp.sum(jnp.where(sub == index, coef, 0.0), axis=0, keepdims=True)


def gram_matrix(sums, index_of):
    sub, lane = iotas((8, 128))
    gram = jnp.zeros((8, 128), F32)
    for a in range(8):
        for b in range(a + 1):
            v = jnp.sum(jnp.sum(sums[a, b], axis=0, keepdims=True), axis=1, keepdims=True)
            i, j = index_of(a), index_of(b)
            here = ((sub == i) & (lane == j)) | ((sub == j) & (lane == i))
            gram = jnp.where(here, v, gram)
    return gram


def kernel(
    x_ref, wt_ref, tgt_ref, table_ref, out_ref,
    X, W, TG, TB, TT, PF, S1, S2, R1, R2, E, G, GA, GB, CS, CB, OWN, AX, AY, AZ,
    loc_sem, w_s, w_r, x_s, x_r, t_s, t_r, y_s, y_r, c_s, c_r, a_s, a_r,
):
    z, x = lax.axis_index("z"), lax.axis_index("x")
    c, y = lax.axis_index("c"), lax.axis_index("shard")

    def zat(d):
        return {"z": lax.rem(z + (d % 8), 8)}

    def yat(d):
        return {"shard": lax.rem(y + (d % 4), 4)}

    def xcat(d, o):
        dev = {}
        if d % 4:
            dev["x"] = lax.rem(x + (d % 4), 4)
        if o:
            dev["c"] = 1 - c
        return dev

    def remote(src, dst, ssem, rsem, dev):
        return pltpu.make_async_remote_copy(
            src_ref=src, dst_ref=dst, send_sem=ssem, recv_sem=rsem, device_id=dev, device_id_type=MESH
        )

    own_x = pltpu.make_async_copy(x_ref, X.at[0], loc_sem.at[8])
    own_x.start()
    blocks = []
    for p in range(8):
        col = lax.rem(z + (DZ[p] % 8), 8) * 512 + x * 128
        cp = pltpu.make_async_copy(
            table_ref.at[:, pl.ds(pl.multiple_of(col, 128), 128)], TB.at[p], loc_sem.at[p]
        )
        cp.start()
        blocks.append(cp)

    barrier = pltpu.get_barrier_semaphore()
    others = [xcat(d, o) for d in range(4) for o in range(2) if d or o]
    others += [yat(d) for d in (1, 2, 3)]
    others += [zat(d) for d in range(1, 8)]
    for dev in others:
        pl.semaphore_signal(barrier, inc=1, device_id=dev, device_id_type=MESH)
    pl.semaphore_wait(barrier, len(others))

    def wslot(ref, d):
        p = block_of(d)
        return ref.at[p // 4, p % 4]

    def wcopy(i):
        n, sign = i // 2 + 1, (1 if i % 2 == 0 else -1)
        src = wt_ref if n == 1 else wslot(W, -sign * (n - 1))
        dst = wslot(W, -sign * n)
        if n == 4:
            rows = pl.ds(0, 32) if sign == 1 else pl.ds(32, 32)
            src, dst = src.at[rows], dst.at[rows]
        return remote(src, dst, w_s.at[i], w_r.at[i], zat(sign))

    wcopies = [wcopy(i) for i in range(8)]
    wcopies[0].start()
    wcopies[1].start()

    lo, hi = pl.ds(0, 160), pl.ds(160, 160)
    xc = [
        remote(X.at[0, lo], X.at[2, lo], x_s.at[0], x_r.at[0], xcat(1, 0)),
        remote(X.at[0, hi], X.at[3, hi], x_s.at[1], x_r.at[1], xcat(-1, 0)),
        remote(X.at[0], X.at[1], x_s.at[2], x_r.at[2], xcat(0, 1)),
        remote(X.at[0, hi], X.at[2, hi], x_s.at[3], x_r.at[3], xcat(1, 0)),
        remote(X.at[0, lo], X.at[3, lo], x_s.at[4], x_r.at[4], xcat(-1, 0)),
        remote(X.at[2, lo], X.at[6, lo], x_s.at[5], x_r.at[5], xcat(1, 0)),
        remote(X.at[3, hi], X.at[6, hi], x_s.at[6], x_r.at[6], xcat(-1, 0)),
        remote(X.at[2], X.at[4], x_s.at[7], x_r.at[7], xcat(0, 1)),
        remote(X.at[3], X.at[5], x_s.at[8], x_r.at[8], xcat(0, 1)),
        remote(X.at[6], X.at[7], x_s.at[9], x_r.at[9], xcat(0, 1)),
    ]
    own_x.wait()
    for i in range(5):
        xc[i].start()

    tcopies = []
    for k in range(1, 8):
        there = place_of(-KX[k], KC[k])
        tc = remote(tgt_ref, TG.at[there], t_s.at[k - 1], t_r.at[there - 1], xcat(KX[k], KC[k]))
        tc.start()
        tcopies.append(tc)
    TG[0] = tgt_ref[...]
    W[0, 0] = wt_ref[...]
    GA[...] = jnp.zeros_like(GA)

    for cp in blocks:
        cp.wait()
    _, lane = iotas((256, 128))
    for q in range(4):
        left = pltpu.roll(TB[2 * q].astype(F32), 64 * c, 1)
        right = pltpu.roll(TB[2 * q + 1].astype(F32), 64 * (1 - c), 1)
        TT[q // 2, :, (q % 2) * 128 : (q % 2) * 128 + 128] = jnp.where(lane < 64, left, right).astype(BF16)

    for tc in tcopies:
        tc.wait()

    for i in (0, 1):
        wcopies[i].wait_recv()
        wcopies[i + 2].start()
    for i in (2, 3):
        wcopies[i].wait_recv()
        wcopies[i + 2].start()

    yp, ym, y2 = lax.rem(y + 1, 4), lax.rem(y + 3, 4), lax.rem(y + 2, 4)

    def unit(u):
        early = u < 4
        k = jnp.where(early, lax.rem(u, 2), u // 2)
        h = jnp.where(early, u // 2, lax.rem(u, 2))
        return k, h

    def r1(u, d):
        return remote(S1.at[u, d], R1.at[u, d], y_s.at[0, d, u], y_r.at[0, d, u], yat(1 - 2 * d))

    def r2(u, d):
        return remote(S2.at[u, d], R2.at[u, d], y_s.at[1, d, u], y_r.at[1, d, u], yat(1 - 2 * d))

    def a1(u, d, who):
        k, h = unit(u)
        ref = E.at[k, h, who]
        return remote(ref, ref, y_s.at[2, d, u], y_r.at[2, d, u], yat(1 - 2 * d))

    def a2(u, d, who):
        k, h = unit(u)
        ref = E.at[k, h, who, :, pl.ds(128 * d, 128)]
        return remote(ref, ref, y_s.at[3, d, u], y_r.at[3, d, u], yat(1 - 2 * d))

    def forward(u):
        k, h = unit(u)
        slot = lax.rem(u, 4)

        @pl.when(u == 1)
        def _():
            xc[2].wait_recv()

        @pl.when(u == 2)
        def _():
            wcopies[6].wait_recv()
            wcopies[7].wait_recv()

        @pl.when(u == 4)
        def _():
            xc[3].wait_recv()
            xc[7].start()

        @pl.when(u == 6)
        def _():
            xc[4].wait_recv()
            xc[8].start()

        @pl.when(u == 8)
        def _():
            xc[7].wait_recv()

        @pl.when(u == 10)
        def _():
            xc[8].wait_recv()

        @pl.when(u == 12)
        def _():
            xc[5].wait_recv()
            xc[6].wait_recv()
            xc[9].start()

        @pl.when(u == 14)
        def _():
            xc[9].wait_recv()

        part = lax.dot_general(
            X[k], W[h].reshape(HALF, FEAT), (((1,), (1,)), ((), ())), preferred_element_type=F32
        )
        PF[slot] = part.reshape(4, PIECE, HALF)
        far = PF[slot, y2].astype(BF16)
        S1[u, 0] = far[:, :128]
        S1[u, 1] = far[:, 128:]
        r1(u, 0).start()
        r1(u, 1).start()
        row = TG[k][0:1]
        sub, _ = iotas((256, 128))
        one_hot = (sub == row).astype(F32).astype(BF16)
        wanted = lax.dot_general(one_hot, TT[h], (((0,), (0,)), ((), ())), preferred_element_type=F32)
        PF[slot, y] = PF[slot, y] - wanted[:PIECE]

        @pl.when(u == 0)
        def _():
            for i in (4, 5):
                wcopies[i].wait_recv()
                wcopies[i + 2].start()

        @pl.when(u == 1)
        def _():
            xc[0].wait_recv()
            xc[5].start()
            xc[1].wait_recv()
            xc[6].start()

    def reduce_step(u):
        slot = lax.rem(u, 4)
        r1(u, 0).wait_recv()
        r1(u, 1).wait_recv()
        S2[u, 0, :, :128] = (PF[slot, yp, :, :128] + R1[u, 0].astype(F32)).astype(BF16)
        S2[u, 0, :, 128:] = PF[slot, yp, :, 128:].astype(BF16)
        r2(u, 0).start()
        S2[u, 1, :, :128] = PF[slot, ym, :, :128].astype(BF16)
        S2[u, 1, :, 128:] = (PF[slot, ym, :, 128:] + R1[u, 1].astype(F32)).astype(BF16)
        r2(u, 1).start()

    def error_step(u):
        k, h = unit(u)
        slot = lax.rem(u, 4)
        r2(u, 0).wait_recv()
        r2(u, 1).wait_recv()
        total = PF[slot, y] + R2[u, 0].astype(F32) + R2[u, 1].astype(F32)
        E[k, h, y] = (total * (1.0 / ROWS)).astype(BF16)
        a1(u, 0, y).start()
        a1(u, 1, y).start()

    def spread_step(u):
        a1(u, 0, ym).wait_recv()
        a2(u, 0, ym).start()
        a1(u, 1, yp).wait_recv()
        a2(u, 1, yp).start()

    def grad_step(u):
        k, h = unit(u)
        a2(u, 0, y2).wait_recv()
        a2(u, 1, y2).wait_recv()
        err = E[k, h].reshape(ROWS, HALF)
        G[k, h] = lax.dot_general(err, X[k], (((0,), (0,)), ((), ())), preferred_element_type=F32)
        for kk in range(8):

            @pl.when(k == kk)
            def _():
                def block(i, sums):
                    rows = pl.ds(pl.multiple_of(i * 8, 8), 8)
                    sums = list(sums)
                    for j in range(FEAT // 128):
                        cols = pl.ds(j * 128, 128)
                        mine = G[kk, h, rows, cols]
                        for l in range(kk):
                            sums[l] = sums[l] + mine * G[l, h, rows, cols]
                        sums[kk] = sums[kk] + mine * mine
                    return tuple(sums)

                sums = lax.fori_loop(
                    0, HALF // 8, block, tuple(jnp.zeros((8, 128), F32) for _ in range(kk + 1))
                )
                for l in range(kk + 1):
                    GA[kk, l] += sums[l]

        for d in range(2):
            r1(u, d).wait_send()
            r2(u, d).wait_send()
            a1(u, d, y).wait_send()
            a2(u, d, ym if d == 0 else yp).wait_send()

    def turn(t, carry):
        @pl.when((t >= 3) & (t < UNITS + 3))
        def _():
            spread_step(t - 3)

        @pl.when((t >= 2) & (t < UNITS + 2))
        def _():
            error_step(t - 2)

        @pl.when((t >= 1) & (t < UNITS + 1))
        def _():
            reduce_step(t - 1)

        @pl.when(t < UNITS)
        def _():
            forward(t)

        @pl.when(t >= 4)
        def _():
            grad_step(t - 4)

        return carry

    lax.fori_loop(0, UNITS + 4, turn, 0)

    def sum_xc(value, s):
        AX[s, 0] = value
        copies = []
        for k in range(1, 8):
            there = place_of(-KX[k], KC[k])
            cp = remote(AX.at[s, 0], AX.at[s, there], a_s.at[s, k], a_r.at[s, there], xcat(KX[k], KC[k]))
            cp.start()
            copies.append(cp)
        for cp in copies:
            cp.wait()
        return functools.reduce(jnp.add, [AX[s, k] for k in range(8)])

    def sum_y(value, s):
        AY[s, 0] = value
        copies = []
        for d in range(1, 4):
            cp = remote(AY.at[s, 0], AY.at[s, 4 - d], a_s.at[2 + s, d], a_r.at[2 + s, 4 - d], yat(d))
            cp.start()
            copies.append(cp)
        for cp in copies:
            cp.wait()
        return functools.reduce(jnp.add, [AY[s, k] for k in range(4)])

    def sum_z(value):
        AZ[0] = value
        copies = []
        for d in range(1, 8):
            cp = remote(AZ.at[0], AZ.at[8 - d], a_s.at[4, d], a_r.at[4, 8 - d], zat(d))
            cp.start()
            copies.append(cp)
        for cp in copies:
            cp.wait()
        return functools.reduce(jnp.add, [AZ[k] for k in range(8)])

    def replica(k):
        return lax.rem(x + (KX[k] % 4), 4) * 2 + lax.rem(c + KC[k], 2)

    coef = tree_coefficients(sum_y(sum_xc(gram_matrix(GA, replica), 0), 0))
    weights = [pick(coef, replica(k)) for k in range(8)]

    ccopies = {}
    for p in (7, 5, 6, 3, 4, 1, 2, 0):

        def mix(i, carry):
            rows = pl.ds(pl.multiple_of((p % 4) * 64 + i * 16, 16), 16)
            total = weights[0] * G[0, p // 4, rows, :]
            for k in range(1, 8):
                total = total + weights[k] * G[k, p // 4, rows, :]
            here = pl.ds(pl.multiple_of(i * 16, 16), 16)
            if p == 0:
                OWN[here, :] = total
            else:
                CS[p, here, :] = total.astype(BF16)
            return carry

        lax.fori_loop(0, 4, mix, 0)
        if p:
            there = block_of(-DZ[p])
            ccopies[there] = remote(CS.at[p], CB.at[there], c_s.at[p], c_r.at[there], zat(DZ[p]))
            ccopies[there].start()

    for p in range(8):
        if p:
            ccopies[p].wait_recv()

        def block(i, sums, p=p):
            rows = pl.ds(pl.multiple_of(i * 16, 16), 16)
            sums = list(sums)
            for j in range(FEAT // 128):
                cols = pl.ds(j * 128, 128)

                def read(q):
                    return CB[q, rows, cols].astype(F32) if q else OWN[rows, cols]

                mine = read(p)
                for l in range(p + 1):
                    prod = mine * read(l)
                    sums[l] = sums[l] + prod[:8] + prod[8:]
            return tuple(sums)

        sums = lax.fori_loop(0, 4, block, tuple(jnp.zeros((8, 128), F32) for _ in range(p + 1)))
        for l in range(p + 1):
            GB[p, l] = sums[l]

    def plane(p):
        return lax.rem(z + (DZ[p] % 8), 8)

    coef = tree_coefficients(sum_z(sum_y(sum_xc(gram_matrix(GB, plane), 1), 1)))
    weights = [pick(coef, plane(p)) for p in range(8)]

    def final(i, carry):
        rows = pl.ds(pl.multiple_of(i * 16, 16), 16)
        total = weights[0] * OWN[rows, :]
        for p in range(1, 8):
            total = total + weights[p] * CB[p, rows, :].astype(F32)
        out_ref[rows, :] = total
        return carry

    lax.fori_loop(0, 4, final, 0)

    for cp in wcopies + xc + list(ccopies.values()):
        cp.wait_send()


def on_device(inputs, weight, table, targets):
    wt = weight.T.astype(BF16)
    tgt = jnp.broadcast_to(jnp.pad(targets, (0, 48))[None], (8, 128))
    vmem = pl.BlockSpec(memory_space=pltpu.VMEM)
    anywhere = pl.BlockSpec(memory_space=pl.ANY)
    dma = pltpu.SemaphoreType.DMA
    combined_t = pl.pallas_call(
        kernel,
        out_shape=jax.ShapeDtypeStruct((64, FEAT), F32),
        in_specs=[anywhere, vmem, vmem, anywhere],
        out_specs=vmem,
        scratch_shapes=[
            pltpu.VMEM((8, ROWS, FEAT), BF16),
            pltpu.VMEM((2, 4, 64, FEAT), BF16),
            pltpu.VMEM((8, 8, 128), jnp.int32),
            pltpu.VMEM((8, 256, 128), BF16),
            pltpu.VMEM((2, 256, HALF), BF16),
            pltpu.VMEM((4, 4, PIECE, HALF), F32),
            pltpu.VMEM((UNITS, 2, PIECE, 128), BF16),
            pltpu.VMEM((UNITS, 2, PIECE, HALF), BF16),
            pltpu.VMEM((UNITS, 2, PIECE, 128), BF16),
            pltpu.VMEM((UNITS, 2, PIECE, HALF), BF16),
            pltpu.VMEM((8, 2, 4, PIECE, HALF), BF16),
            pltpu.VMEM((8, 2, HALF, FEAT), F32),
            pltpu.VMEM((8, 8, 8, 128), F32),
            pltpu.VMEM((8, 8, 8, 128), F32),
            pltpu.VMEM((8, 64, FEAT), BF16),
            pltpu.VMEM((8, 64, FEAT), BF16),
            pltpu.VMEM((64, FEAT), F32),
            pltpu.VMEM((2, 8, 8, 128), F32),
            pltpu.VMEM((2, 4, 8, 128), F32),
            pltpu.VMEM((8, 8, 128), F32),
            dma((9,)),
            dma((8,)),
            dma((8,)),
            dma((10,)),
            dma((10,)),
            dma((7,)),
            dma((7,)),
            dma((4, 2, UNITS)),
            dma((4, 2, UNITS)),
            dma((8,)),
            dma((8,)),
            dma((5, 8)),
            dma((5, 8)),
        ],
        compiler_params=pltpu.CompilerParams(
            collective_id=0, has_side_effects=True, vmem_limit_bytes=56 * 1024 * 1024
        ),
    )(inputs, wt, tgt, table)
    combined = combined_t.T
    return combined, weight - STEP * combined


def solution(mesh):
    split = Mesh(mesh.devices.reshape(8, 4, 2, mesh.shape["shard"]), AXES)
    return jax.shard_map(
        on_device,
        mesh=split,
        in_specs=(P(REP, "shard"), P("shard", REP), P(), P(REP + ("shard",))),
        out_specs=(P("shard", REP), P("shard", REP)),
        check_vma=False,
    )
```

time: 771 us -> 171 us (0.22)
  waiting for transfers between devices: 386 us -> 0 us
  blocking collectives: 215 us -> 0 us
  Pallas kernels: 0 us -> 164 us
  other arithmetic: 103 us -> 3.3 us
  between operations: 31.4 us -> 0.66 us
  matrix products: 18.8 us -> 0 us
  starting transfers between devices: 9.92 us -> 0 us
    psum x24 -> x0, blocking collectives: 215 us -> none  [over_axes(): return functools.reduce(lax.psum, axes, shard)]
    ppermute x6 -> x0, waiting for transfers between devices: 211 us -> none  [from_partner(): return lax.ppermute(block, axis, route)]
    pallas_call x0 -> x1, Pallas kernels: none -> 164 us  [on_device(): pl.pallas_call(kernel, out_shape=jax.ShapeDtypeStruct((64, FEAT), F32), i...]
    all_gather x1 -> x0, waiting for transfers between devices: 89.5 us -> none  [on_device(): lax.all_gather(weight.astype(jnp.bfloat16), REP, axis=1, tiled=True)]
    reduce_scatter x1 -> x0, waiting for transfers between devices: 53.4 us -> none  [on_device(): lax.psum_scatter(jnp.dot(row_block, weight_full, preferred_element_type=j...]
    reduce_sum x21 -> x0, other arithmetic: 46 us -> none  [the longest x6 36.9 us: on_device(): jnp.sum(lower_vec * lower_vec)]
    all_to_all x1 -> x0, waiting for transfers between devices: 31.4 us -> none  [from_everyone(): lax.all_to_all(jnp.broadcast_to(shard[None], (peers, *shard.shape)), axis...]
    select_n x7 -> x0, other arithmetic: 21.3 us -> none  [the longest x6 21.3 us: on_device(): outgoing = jnp.where(own_bit == 1, halves[:, :, 0], halves[:, :, 1])]
  transfers between devices with their start and end apart: 9 -> 0, of which waited for: 9 -> 0; matrix products, arithmetic and copies ran while one was open for 0% -> 0% of each run, Pallas kernels for 0% -> 0%
where the time goes in v1:
time: 171 us
  Pallas kernels  164 us (96%)
  other arithmetic  3.3 us (2%)
  local copies, waits for them, and re-layouts  2.97 us (2%)
    pallas_call x1, Pallas kernels, on_device(): pl.pallas_call(kernel, out_shape=jax.ShapeDtypeStruct((64, FEAT), F32), i...  164 us

profile of v1, /device:TPU:1, one launch (start us, length us, event | category | flops | bytes accessed | tf_op | source)
XLA Modules:
  0.0 170.9 jit_solution(9123349450981069338)
XLA Ops:
  0.6 0.0 copy-start
  0.6 0.7 pad.4
  1.3 0.6 broadcast_in_dim.2.tgt_ref
  1.9 1.6 convert_bitcast_fusion.wt_ref
  3.6 164.0 %shard_map.59 = f32[64,1024]{1,0:T(8,128)} custom-call(bf16[320,1024]{1,0:T(8,128)(2,1)} %x_ref.1, bf16[64,1024]{1,0:T(8,128)(2,1)} %convert_bitcast_fusion.wt_ref, s32[8,128]{1,0:T(8,128)} %broadcast_in_dim.2.tgt_ref, bf16[256,4096]{1,0:T(8,128)(2,1)} %table_ref.1), custom_call_target="tpu_custom_call" | custom-call | tf_op jit(solution)/shard_map/pallas_call | solution.py:478
  167.6 0.0 copy-done
  167.6 1.7 multiply_subtract_fusion
  169.3 1.7 copy.7
Async XLA Ops:
  0.6 166.9 %copy-start = (f32[1024,64]{0,1:T(8,128)S(1)}, f32[1024,64]{0,1:T(8,128)}, u32[]{:S(2)}) copy-start(f32[1024,64]{0,1:T(8,128)} %param.5) | copy-start | bytes 786436

commit v2 on v1

--- a/solution.py
+++ b/solution.py
@@ -21,7 +21,7 @@
 DZ = (0, -1, 1, -2, 2, -3, 3, 4)
 
 ROWS, FEAT, PIECE, HALF = 320, 1024, 80, 256
-UNITS = 16
+UNITS, LAG = 16, 2
 
 
 def place_of(steps, other):
@@ -80,7 +80,7 @@
 
 
 def kernel(
-    x_ref, wt_ref, tgt_ref, table_ref, out_ref,
+    x_ref, w_ref, tgt_ref, table_ref, out_ref,
     X, W, TG, TB, TT, PF, S1, S2, R1, R2, E, G, GA, GB, CS, CB, OWN, AX, AY, AZ,
     loc_sem, w_s, w_r, x_s, x_r, t_s, t_r, y_s, y_r, c_s, c_r, a_s, a_r,
 ):
@@ -105,6 +105,9 @@
         return pltpu.make_async_remote_copy(
             src_ref=src, dst_ref=dst, send_sem=ssem, recv_sem=rsem, device_id=dev, device_id_type=MESH
         )
+
+    TG[0] = jnp.zeros((8, 128), jnp.int32)
+    TG[0, 0:1, 0:PIECE] = tgt_ref[...]
 
     own_x = pltpu.make_async_copy(x_ref, X.at[0], loc_sem.at[8])
     own_x.start()
@@ -125,22 +128,23 @@
         pl.semaphore_signal(barrier, inc=1, device_id=dev, device_id_type=MESH)
     pl.semaphore_wait(barrier, len(others))
 
-    def wslot(ref, d):
+    def wslot(d):
         p = block_of(d)
-        return ref.at[p // 4, p % 4]
+        return W.at[p // 4, p % 4]
 
     def wcopy(i):
         n, sign = i // 2 + 1, (1 if i % 2 == 0 else -1)
-        src = wt_ref if n == 1 else wslot(W, -sign * (n - 1))
-        dst = wslot(W, -sign * n)
+        src = wslot(0) if n <= 2 else wslot(-sign * 2)
+        dst = wslot(-sign * n)
         if n == 4:
             rows = pl.ds(0, 32) if sign == 1 else pl.ds(32, 32)
             src, dst = src.at[rows], dst.at[rows]
-        return remote(src, dst, w_s.at[i], w_r.at[i], zat(sign))
-
+        return remote(src, dst, w_s.at[i], w_r.at[i], zat(sign * (n if n <= 2 else n - 2)))
+
+    W[0, 0] = w_ref[...].astype(BF16)
     wcopies = [wcopy(i) for i in range(8)]
-    wcopies[0].start()
-    wcopies[1].start()
+    for i in range(4):
+        wcopies[i].start()
 
     lo, hi = pl.ds(0, 160), pl.ds(160, 160)
     xc = [
@@ -162,11 +166,9 @@
     tcopies = []
     for k in range(1, 8):
         there = place_of(-KX[k], KC[k])
-        tc = remote(tgt_ref, TG.at[there], t_s.at[k - 1], t_r.at[there - 1], xcat(KX[k], KC[k]))
+        tc = remote(TG.at[0], TG.at[there], t_s.at[k - 1], t_r.at[there - 1], xcat(KX[k], KC[k]))
         tc.start()
         tcopies.append(tc)
-    TG[0] = tgt_ref[...]
-    W[0, 0] = wt_ref[...]
     GA[...] = jnp.zeros_like(GA)
 
     for cp in blocks:
@@ -182,10 +184,10 @@
 
     for i in (0, 1):
         wcopies[i].wait_recv()
-        wcopies[i + 2].start()
     for i in (2, 3):
         wcopies[i].wait_recv()
         wcopies[i + 2].start()
+        wcopies[i + 4].start()
 
     yp, ym, y2 = lax.rem(y + 1, 4), lax.rem(y + 3, 4), lax.rem(y + 2, 4)
 
@@ -213,7 +215,7 @@
 
     def forward(u):
         k, h = unit(u)
-        slot = lax.rem(u, 4)
+        slot = lax.rem(u, 8)
 
         @pl.when(u == 1)
         def _():
@@ -221,8 +223,8 @@
 
         @pl.when(u == 2)
         def _():
-            wcopies[6].wait_recv()
-            wcopies[7].wait_recv()
+            for i in (4, 5, 6, 7):
+                wcopies[i].wait_recv()
 
         @pl.when(u == 4)
         def _():
@@ -267,12 +269,6 @@
         wanted = lax.dot_general(one_hot, TT[h], (((0,), (0,)), ((), ())), preferred_element_type=F32)
         PF[slot, y] = PF[slot, y] - wanted[:PIECE]
 
-        @pl.when(u == 0)
-        def _():
-            for i in (4, 5):
-                wcopies[i].wait_recv()
-                wcopies[i + 2].start()
-
         @pl.when(u == 1)
         def _():
             xc[0].wait_recv()
@@ -281,7 +277,7 @@
             xc[6].start()
 
     def reduce_step(u):
-        slot = lax.rem(u, 4)
+        slot = lax.rem(u, 8)
         r1(u, 0).wait_recv()
         r1(u, 1).wait_recv()
         S2[u, 0, :, :128] = (PF[slot, yp, :, :128] + R1[u, 0].astype(F32)).astype(BF16)
@@ -293,7 +289,7 @@
 
     def error_step(u):
         k, h = unit(u)
-        slot = lax.rem(u, 4)
+        slot = lax.rem(u, 8)
         r2(u, 0).wait_recv()
         r2(u, 1).wait_recv()
         total = PF[slot, y] + R2[u, 0].astype(F32) + R2[u, 1].astype(F32)
@@ -341,29 +337,15 @@
             a2(u, d, ym if d == 0 else yp).wait_send()
 
     def turn(t, carry):
-        @pl.when((t >= 3) & (t < UNITS + 3))
-        def _():
-            spread_step(t - 3)
-
-        @pl.when((t >= 2) & (t < UNITS + 2))
-        def _():
-            error_step(t - 2)
-
-        @pl.when((t >= 1) & (t < UNITS + 1))
-        def _():
-            reduce_step(t - 1)
-
-        @pl.when(t < UNITS)
-        def _():
-            forward(t)
-
-        @pl.when(t >= 4)
-        def _():
-            grad_step(t - 4)
+        for n, step in ((3, spread_step), (2, error_step), (1, reduce_step), (0, forward), (4, grad_step)):
+
+            @pl.when((t >= n * LAG) & (t < UNITS + n * LAG))
+            def _():
+                step(t - n * LAG)
 
         return carry
 
-    lax.fori_loop(0, UNITS + 4, turn, 0)
+    lax.fori_loop(0, UNITS + 4 * LAG, turn, 0)
 
     def sum_xc(value, s):
         AX[s, 0] = value
@@ -470,8 +452,6 @@
 
 
 def on_device(inputs, weight, table, targets):
-    wt = weight.T.astype(BF16)
-    tgt = jnp.broadcast_to(jnp.pad(targets, (0, 48))[None], (8, 128))
     vmem = pl.BlockSpec(memory_space=pltpu.VMEM)
     anywhere = pl.BlockSpec(memory_space=pl.ANY)
     dma = pltpu.SemaphoreType.DMA
@@ -486,7 +466,7 @@
             pltpu.VMEM((8, 8, 128), jnp.int32),
             pltpu.VMEM((8, 256, 128), BF16),
             pltpu.VMEM((2, 256, HALF), BF16),
-            pltpu.VMEM((4, 4, PIECE, HALF), F32),
+            pltpu.VMEM((8, 4, PIECE, HALF), F32),
             pltpu.VMEM((UNITS, 2, PIECE, 128), BF16),
             pltpu.VMEM((UNITS, 2, PIECE, HALF), BF16),
             pltpu.VMEM((UNITS, 2, PIECE, 128), BF16),
@@ -518,7 +498,7 @@
         compiler_params=pltpu.CompilerParams(
             collective_id=0, has_side_effects=True, vmem_limit_bytes=56 * 1024 * 1024
         ),
-    )(inputs, wt, tgt, table)
+    )(inputs, weight.T, targets[None], table)
     combined = combined_t.T
     return combined, weight - STEP * combined
 

time: 171 us -> 137 us (0.80)
  Pallas kernels: 164 us -> 133 us
    pallas_call x1, Pallas kernels: 164 us -> 133 us  [on_device(): pl.pallas_call(kernel, out_shape=jax.ShapeDtypeStruct((64, FEAT), F32), i...]
where the time goes in v2:
time: 137 us
  Pallas kernels  133 us (97%)
  other arithmetic  1.69 us (1%)
  local copies, waits for them, and re-layouts  1.67 us (1%)
    pallas_call x1, Pallas kernels, on_device(): pl.pallas_call(kernel, out_shape=jax.ShapeDtypeStruct((64, FEAT), F32), i...  133 us

profile of v2, /device:TPU:1, one launch (start us, length us, event | category | flops | bytes accessed | tf_op | source)
XLA Modules:
  0.0 136.9 jit_solution(3247772714711441587)
XLA Ops:
  0.6 0.0 copy-start
  0.6 132.9 %shard_map.59 = f32[64,1024]{1,0:T(8,128)} custom-call(bf16[320,1024]{1,0:T(8,128)(2,1)} %x_ref.1, f32[64,1024]{1,0:T(8,128)} %bitcast.5, s32[1,80]{1,0:T(1,128)} %bitcast.6, bf16[256,4096]{1,0:T(8,128)(2,1)} %table_ref.1), custom_call_target="tpu_custom_call" | custom-call | tf_op jit(solution)/shard_map/pallas_call | solution.py:458
  133.5 0.0 copy-done
  133.5 1.7 %multiply_subtract_fusion = f32[1024,64]{0,1:T(8,128)} fusion(f32[1024,64]{0,1:T(8,128)S(1)} %copy-done, f32[64,1024]{1,0:T(8,128)} %shard_map.59), kind=kLoop, calls=%fused_computation | loop fusion | flops 131072 | bytes 786432 | tf_op jit(solution)/shard_map/sub | solution.py:503
  135.2 1.7 %copy.7 = f32[1024,64]{0,1:T(8,128)} copy(f32[1024,64]{0,1:T(8,128)} %bitcast.4) | data formatting | bytes 524288
Async XLA Ops:
  0.6 132.9 %copy-start = (f32[1024,64]{0,1:T(8,128)S(1)}, f32[1024,64]{0,1:T(8,128)}, u32[]{:S(2)}) copy-start(f32[1024,64]{0,1:T(8,128)} %param.5) | copy-start | bytes 786436

commit v3 on v2

--- a/solution.py
+++ b/solution.py
@@ -80,8 +80,8 @@
 
 
 def kernel(
-    x_ref, w_ref, tgt_ref, table_ref, out_ref,
-    X, W, TG, TB, TT, PF, S1, S2, R1, R2, E, G, GA, GB, CS, CB, OWN, AX, AY, AZ,
+    x_ref, w_ref, tgt_ref, table_ref, near_ref, far_ref,
+    X, W, TG, TB, TT, PF, S1, S2, R1, R2, E, G, GA, GB, CS, CB, OWN, AC, AX, AZ,
     loc_sem, w_s, w_r, x_s, x_r, t_s, t_r, y_s, y_r, c_s, c_r, a_s, a_r,
 ):
     z, x = lax.axis_index("z"), lax.axis_index("x")
@@ -101,11 +101,20 @@
             dev["c"] = 1 - c
         return dev
 
+    def xyat(d, e):
+        return {"x": lax.rem(x + (d % 4), 4), "shard": lax.rem(y + (e % 4), 4)}
+
     def remote(src, dst, ssem, rsem, dev):
         return pltpu.make_async_remote_copy(
             src_ref=src, dst_ref=dst, send_sem=ssem, recv_sem=rsem, device_id=dev, device_id_type=MESH
         )
 
+    barrier = pltpu.get_barrier_semaphore()
+    others = [zat(d) for d in (4, 3, 5, 2, 6, 1, 7)]
+    others += [xyat(d, e) for d in range(4) for e in range(4) if d or e]
+    others += [xcat(d, 1) for d in range(4)]
+    for dev in others:
+        pl.semaphore_signal(barrier, inc=1, device_id=dev, device_id_type=MESH)
     TG[0] = jnp.zeros((8, 128), jnp.int32)
     TG[0, 0:1, 0:PIECE] = tgt_ref[...]
 
@@ -120,12 +129,18 @@
         cp.start()
         blocks.append(cp)
 
-    barrier = pltpu.get_barrier_semaphore()
-    others = [xcat(d, o) for d in range(4) for o in range(2) if d or o]
-    others += [yat(d) for d in (1, 2, 3)]
-    others += [zat(d) for d in range(1, 8)]
-    for dev in others:
-        pl.semaphore_signal(barrier, inc=1, device_id=dev, device_id_type=MESH)
+    W[0, 0] = w_ref[...].astype(BF16)
+    GA[...] = jnp.zeros_like(GA)
+
+    for cp in blocks:
+        cp.wait()
+    _, lane = iotas((256, 128))
+    for q in range(4):
+        left = pltpu.roll(TB[2 * q].astype(F32), 64 * c, 1)
+        right = pltpu.roll(TB[2 * q + 1].astype(F32), 64 * (1 - c), 1)
+        TT[q // 2, :, (q % 2) * 128 : (q % 2) * 128 + 128] = jnp.where(lane < 64, left, right).astype(BF16)
+
+    own_x.wait()
     pl.semaphore_wait(barrier, len(others))
 
     def wslot(d):
@@ -141,7 +156,6 @@
             src, dst = src.at[rows], dst.at[rows]
         return remote(src, dst, w_s.at[i], w_r.at[i], zat(sign * (n if n <= 2 else n - 2)))
 
-    W[0, 0] = w_ref[...].astype(BF16)
     wcopies = [wcopy(i) for i in range(8)]
     for i in range(4):
         wcopies[i].start()
@@ -159,7 +173,6 @@
         remote(X.at[3], X.at[5], x_s.at[8], x_r.at[8], xcat(0, 1)),
         remote(X.at[6], X.at[7], x_s.at[9], x_r.at[9], xcat(0, 1)),
     ]
-    own_x.wait()
     for i in range(5):
         xc[i].start()
 
@@ -169,16 +182,6 @@
         tc = remote(TG.at[0], TG.at[there], t_s.at[k - 1], t_r.at[there - 1], xcat(KX[k], KC[k]))
         tc.start()
         tcopies.append(tc)
-    GA[...] = jnp.zeros_like(GA)
-
-    for cp in blocks:
-        cp.wait()
-    _, lane = iotas((256, 128))
-    for q in range(4):
-        left = pltpu.roll(TB[2 * q].astype(F32), 64 * c, 1)
-        right = pltpu.roll(TB[2 * q + 1].astype(F32), 64 * (1 - c), 1)
-        TT[q // 2, :, (q % 2) * 128 : (q % 2) * 128 + 128] = jnp.where(lane < 64, left, right).astype(BF16)
-
     for tc in tcopies:
         tc.wait()
 
@@ -269,7 +272,7 @@
         wanted = lax.dot_general(one_hot, TT[h], (((0,), (0,)), ((), ())), preferred_element_type=F32)
         PF[slot, y] = PF[slot, y] - wanted[:PIECE]
 
-        @pl.when(u == 1)
+        @pl.when(u == 3)
         def _():
             xc[0].wait_recv()
             xc[5].start()
@@ -347,34 +350,28 @@
 
     lax.fori_loop(0, UNITS + 4 * LAG, turn, 0)
 
-    def sum_xc(value, s):
-        AX[s, 0] = value
+    def sum_plane(value, s):
+        AC[s, 0] = value
+        cp = remote(AC.at[s, 0], AC.at[s, 1], a_s.at[s, 0], a_r.at[s, 0], xcat(0, 1))
+        cp.start()
+        cp.wait()
+        AX[s, 0] = AC[s, 0] + AC[s, 1]
         copies = []
-        for k in range(1, 8):
-            there = place_of(-KX[k], KC[k])
-            cp = remote(AX.at[s, 0], AX.at[s, there], a_s.at[s, k], a_r.at[s, there], xcat(KX[k], KC[k]))
+        for i in range(1, 16):
+            d, e = i // 4, i % 4
+            there = (-d) % 4 * 4 + (-e) % 4
+            cp = remote(AX.at[s, 0], AX.at[s, there], a_s.at[s, i], a_r.at[s, there], xyat(d, e))
             cp.start()
             copies.append(cp)
         for cp in copies:
             cp.wait()
-        return functools.reduce(jnp.add, [AX[s, k] for k in range(8)])
-
-    def sum_y(value, s):
-        AY[s, 0] = value
-        copies = []
-        for d in range(1, 4):
-            cp = remote(AY.at[s, 0], AY.at[s, 4 - d], a_s.at[2 + s, d], a_r.at[2 + s, 4 - d], yat(d))
-            cp.start()
-            copies.append(cp)
-        for cp in copies:
-            cp.wait()
-        return functools.reduce(jnp.add, [AY[s, k] for k in range(4)])
+        return jnp.sum(AX[s], axis=0)
 
     def sum_z(value):
         AZ[0] = value
         copies = []
         for d in range(1, 8):
-            cp = remote(AZ.at[0], AZ.at[8 - d], a_s.at[4, d], a_r.at[4, 8 - d], zat(d))
+            cp = remote(AZ.at[0], AZ.at[8 - d], a_s.at[2, d], a_r.at[2, 8 - d], zat(d))
             cp.start()
             copies.append(cp)
         for cp in copies:
@@ -384,7 +381,7 @@
     def replica(k):
         return lax.rem(x + (KX[k] % 4), 4) * 2 + lax.rem(c + KC[k], 2)
 
-    coef = tree_coefficients(sum_y(sum_xc(gram_matrix(GA, replica), 0), 0))
+    coef = tree_coefficients(sum_plane(gram_matrix(GA, replica), 0))
     weights = [pick(coef, replica(k)) for k in range(8)]
 
     ccopies = {}
@@ -434,15 +431,19 @@
     def plane(p):
         return lax.rem(z + (DZ[p] % 8), 8)
 
-    coef = tree_coefficients(sum_z(sum_y(sum_xc(gram_matrix(GB, plane), 1), 1)))
+    coef = tree_coefficients(sum_z(sum_plane(gram_matrix(GB, plane), 1)))
     weights = [pick(coef, plane(p)) for p in range(8)]
 
     def final(i, carry):
         rows = pl.ds(pl.multiple_of(i * 16, 16), 16)
-        total = weights[0] * OWN[rows, :]
-        for p in range(1, 8):
-            total = total + weights[p] * CB[p, rows, :].astype(F32)
-        out_ref[rows, :] = total
+        near = weights[0] * OWN[rows, :]
+        for p in range(1, 4):
+            near = near + weights[p] * CB[p, rows, :].astype(F32)
+        far = weights[4] * CB[4, rows, :].astype(F32)
+        for p in range(5, 8):
+            far = far + weights[p] * CB[p, rows, :].astype(F32)
+        near_ref[rows, :] = near
+        far_ref[rows, :] = far
         return carry
 
     lax.fori_loop(0, 4, final, 0)
@@ -455,11 +456,11 @@
     vmem = pl.BlockSpec(memory_space=pltpu.VMEM)
     anywhere = pl.BlockSpec(memory_space=pl.ANY)
     dma = pltpu.SemaphoreType.DMA
-    combined_t = pl.pallas_call(
+    near, far = pl.pallas_call(
         kernel,
-        out_shape=jax.ShapeDtypeStruct((64, FEAT), F32),
+        out_shape=[jax.ShapeDtypeStruct((64, FEAT), F32)] * 2,
         in_specs=[anywhere, vmem, vmem, anywhere],
-        out_specs=vmem,
+        out_specs=[vmem] * 2,
         scratch_shapes=[
             pltpu.VMEM((8, ROWS, FEAT), BF16),
             pltpu.VMEM((2, 4, 64, FEAT), BF16),
@@ -478,8 +479,8 @@
             pltpu.VMEM((8, 64, FEAT), BF16),
             pltpu.VMEM((8, 64, FEAT), BF16),
             pltpu.VMEM((64, FEAT), F32),
-            pltpu.VMEM((2, 8, 8, 128), F32),
-            pltpu.VMEM((2, 4, 8, 128), F32),
+            pltpu.VMEM((2, 2, 8, 128), F32),
+            pltpu.VMEM((2, 16, 8, 128), F32),
             pltpu.VMEM((8, 8, 128), F32),
             dma((9,)),
             dma((8,)),
@@ -492,15 +493,15 @@
             dma((4, 2, UNITS)),
             dma((8,)),
             dma((8,)),
-            dma((5, 8)),
-            dma((5, 8)),
+            dma((3, 16)),
+            dma((3, 16)),
         ],
         compiler_params=pltpu.CompilerParams(
             collective_id=0, has_side_effects=True, vmem_limit_bytes=56 * 1024 * 1024
         ),
     )(inputs, weight.T, targets[None], table)
-    combined = combined_t.T
-    return combined, weight - STEP * combined
+    combined = near + far
+    return combined.T, (weight.T - STEP * combined).T
 
 
 def solution(mesh):

time: 137 us -> 134 us (0.978)
  Pallas kernels: 133 us -> 131 us
  local copies, waits for them, and re-layouts: 1.67 us -> 0.01 us
    transpose x0 -> x1, other arithmetic: none -> 1.88 us  [on_device(): return (combined.T, (weight.T - STEP * combined).T)]
    sub x1 -> x0, other arithmetic: 1.69 us -> none  [on_device(): return (combined, weight - STEP * combined)]
    unnamed x3 -> x2, local copies, waits for them, and re-layouts: 1.67 us -> 0.01 us
    pallas_call x1, Pallas kernels: 133 us -> 131 us  [on_device(): pl.pallas_call(kernel, out_shape=[jax.ShapeDtypeStruct((64, FEAT), F32)]...]
where the time goes in v3:
time: 134 us
  Pallas kernels  131 us (98%)
  other arithmetic  1.88 us (1%)
    pallas_call x1, Pallas kernels, on_device(): pl.pallas_call(kernel, out_shape=[jax.ShapeDtypeStruct((64, FEAT), F32)]...  131 us

profile of v3, /device:TPU:1, one launch (start us, length us, event | category | flops | bytes accessed | tf_op | source)
XLA Modules:
  0.0 133.9 jit_solution(10372771575012974319)
XLA Ops:
  0.6 0.0 copy-start
  0.6 131.4 %shard_map.59 = (f32[64,1024]{1,0:T(8,128)}, f32[64,1024]{1,0:T(8,128)}) custom-call(bf16[320,1024]{1,0:T(8,128)(2,1)} %x_ref.1, f32[64,1024]{1,0:T(8,128)} %bitcast.7, s32[1,80]{1,0:T(1,128)} %bitcast.8, bf16[256,4096]{1,0:T(8,128)(2,1)} %table_ref.1), custom_call_target="tpu_custom_call" | custom-call | tf_op jit(solution)/shard_map/pallas_call | solution.py:459
  132.1 0.0 copy-done
  132.1 1.9 %subtract_bitcast_fusion = (f32[1024,64]{0,1:T(8,128)}, f32[1024,64]{0,1:T(8,128)}) fusion(f32[64,1024]{1,0:T(8,128)} %get-tuple-element.4, f32[64,1024]{1,0:T(8,128)} %get-tuple-element.5, f32[1024,64]{0,1:T(8,128)S(1)} %copy-done), kind=kLoop, calls=%fused_computation | loop fusion | flops 196608 | bytes 1310720 | tf_op jit(solution)/shard_map/transpose | solution.py:504
Async XLA Ops:
  0.6 131.4 %copy-start = (f32[1024,64]{0,1:T(8,128)S(1)}, f32[1024,64]{0,1:T(8,128)}, u32[]{:S(2)}) copy-start(f32[1024,64]{0,1:T(8,128)} %param.5) | copy-start | bytes 786436

commit v4 on v3

--- a/solution.py
+++ b/solution.py
@@ -143,6 +143,12 @@
     own_x.wait()
     pl.semaphore_wait(barrier, len(others))
 
+    tcopies = []
+    for k in range(1, 8):
+        there = place_of(-KX[k], KC[k])
+        tc = remote(TG.at[0], TG.at[there], t_s.at[k - 1], t_r.at[there - 1], xcat(KX[k], KC[k]))
+        tc.start()
+        tcopies.append(tc)
     def wslot(d):
         p = block_of(d)
         return W.at[p // 4, p % 4]
@@ -176,15 +182,6 @@
     for i in range(5):
         xc[i].start()
 
-    tcopies = []
-    for k in range(1, 8):
-        there = place_of(-KX[k], KC[k])
-        tc = remote(TG.at[0], TG.at[there], t_s.at[k - 1], t_r.at[there - 1], xcat(KX[k], KC[k]))
-        tc.start()
-        tcopies.append(tc)
-    for tc in tcopies:
-        tc.wait()
-
     for i in (0, 1):
         wcopies[i].wait_recv()
     for i in (2, 3):
@@ -266,6 +263,12 @@
         S1[u, 1] = far[:, 128:]
         r1(u, 0).start()
         r1(u, 1).start()
+
+        @pl.when(u == 0)
+        def _():
+            for tc in tcopies:
+                tc.wait()
+
         row = TG[k][0:1]
         sub, _ = iotas((256, 128))
         one_hot = (sub == row).astype(F32).astype(BF16)

time: 134 us -> 127 us (0.948)
  Pallas kernels: 131 us -> 124 us
    pallas_call x1, Pallas kernels: 131 us -> 124 us  [on_device(): pl.pallas_call(kernel, out_shape=[jax.ShapeDtypeStruct((64, FEAT), F32)]...]
where the time goes in v4:
time: 127 us
  Pallas kernels  124 us (98%)
  other arithmetic  1.88 us (1%)
    pallas_call x1, Pallas kernels, on_device(): pl.pallas_call(kernel, out_shape=[jax.ShapeDtypeStruct((64, FEAT), F32)]...  124 us

profile of v4, /device:TPU:1, one launch (start us, length us, event | category | flops | bytes accessed | tf_op | source)
XLA Modules:
  0.0 126.9 jit_solution(13684362706669656742)
XLA Ops:
  0.6 0.0 copy-start
  0.6 124.4 %shard_map.59 = (f32[64,1024]{1,0:T(8,128)}, f32[64,1024]{1,0:T(8,128)}) custom-call(bf16[320,1024]{1,0:T(8,128)(2,1)} %x_ref.1, f32[64,1024]{1,0:T(8,128)} %bitcast.7, s32[1,80]{1,0:T(1,128)} %bitcast.8, bf16[256,4096]{1,0:T(8,128)(2,1)} %table_ref.1), custom_call_target="tpu_custom_call" | custom-call | tf_op jit(solution)/shard_map/pallas_call | solution.py:462
  125.0 0.0 copy-done
  125.0 1.9 %subtract_bitcast_fusion = (f32[1024,64]{0,1:T(8,128)}, f32[1024,64]{0,1:T(8,128)}) fusion(f32[64,1024]{1,0:T(8,128)} %get-tuple-element.4, f32[64,1024]{1,0:T(8,128)} %get-tuple-element.5, f32[1024,64]{0,1:T(8,128)S(1)} %copy-done), kind=kLoop, calls=%fused_computation | loop fusion | flops 196608 | bytes 1310720 | tf_op jit(solution)/shard_map/transpose | solution.py:507
Async XLA Ops:
  0.6 124.4 %copy-start = (f32[1024,64]{0,1:T(8,128)S(1)}, f32[1024,64]{0,1:T(8,128)}, u32[]{:S(2)}) copy-start(f32[1024,64]{0,1:T(8,128)} %param.5) | copy-start | bytes 786436

commit v5 on v4

v5 whole, which is shorter than its diff:
```python
import functools

import jax
import jax.numpy as jnp
from jax import lax
from jax.experimental import pallas as pl
from jax.experimental.pallas import tpu as pltpu
from jax.sharding import Mesh
from jax.sharding import PartitionSpec as P

AXES = ("z", "x", "c", "shard")
REP = ("z", "x", "c")
MESH = pl.DeviceIdType.MESH
F32, BF16 = jnp.float32, jnp.bfloat16

EPS = 1e-06
STEP = 0.05

KX = (0, 0, -1, 1, -1, 1, 0, 0, 2, 2, -1, 1, -1, 1, 2, 2)
KC = (0, 1, 0, 0, 1, 1, 0, 1, 0, 1, 0, 0, 1, 1, 0, 1)
KM = (0, 0, 0, 0, 0, 0, 1, 1, 0, 0, 1, 1, 1, 1, 1, 1)
DZ = (0, 2, -2, 4)

ROWS, FEAT, PIECE, HALF = 320, 1024, 80, 256
UNITS, LAG = 16, 2


def place_of(steps, other, plane):
    return [i for i in range(16) if (KX[i] % 4, KC[i], KM[i]) == (steps % 4, other, plane)][0]


def block_of(steps):
    return [i for i in range(4) if DZ[i] % 8 == steps % 8][0]


def iotas(shape):
    return lax.broadcasted_iota(jnp.int32, shape, 0), lax.broadcasted_iota(jnp.int32, shape, 1)


def swap_bit(v, bit, axis):
    pos = lax.broadcasted_iota(jnp.int32, v.shape, axis)
    up = pltpu.roll(v, bit, axis)
    down = pltpu.roll(v, v.shape[axis] - bit, axis)
    return jnp.where((pos & bit) != 0, up, down)


def tree_coefficients(gram, bits):
    sub, lane = iotas(gram.shape)
    coef = jnp.ones((gram.shape[0], 1), F32)
    for bit in bits:
        own = jnp.where(lane == sub, gram, 0.0)
        cross = jnp.where(lane == (sub ^ bit), gram, 0.0)

        def factor(axis):
            norm = jnp.maximum(jnp.sum(own, axis=axis, keepdims=True), 0.0)
            return 1.0 - jnp.sum(cross, axis=axis, keepdims=True) / (2.0 * (norm + EPS))

        by_row, by_col = factor(1), factor(0)
        coef = coef * by_row
        gram = gram * by_row * by_col
        gram = gram + swap_bit(gram, bit, 1)
        gram = gram + swap_bit(gram, bit, 0)
    return coef


def pick(coef, index):
    sub, _ = iotas(coef.shape)
    return jnp.sum(jnp.where(sub == index, coef, 0.0), axis=0, keepdims=True)


def put_pair(gram, i, j, products):
    sub, lane = iotas(gram.shape)
    v = jnp.sum(jnp.sum(products, axis=0, keepdims=True), axis=1, keepdims=True)
    return jnp.where(((sub == i) & (lane == j)) | ((sub == j) & (lane == i)), v, gram)


def kernel(
    x_ref, w_ref, tgt_ref, table_ref, near_ref, far_ref,
    X, W, TG, TB, TT, PF, S1, S2, R1, R2, E, G, GA, CS, CB, OWN, AC, AX, BC, BX, AZ,
    loc_sem, w_s, w_r, z_s, z_r, x_s, x_r, t_s, t_r, y_s, y_r, c_s, c_r, a_s, a_r,
):
    z, x = lax.axis_index("z"), lax.axis_index("x")
    c, y = lax.axis_index("c"), lax.axis_index("shard")

    def zat(d):
        return {"z": lax.rem(z + (d % 8), 8)}

    def yat(d):
        return {"shard": lax.rem(y + (d % 4), 4)}

    def xcat(d, o):
        dev = {}
        if d % 4:
            dev["x"] = lax.rem(x + (d % 4), 4)
        if o:
            dev["c"] = 1 - c
        return dev

    mine = lax.rem(z, 2)

    def partner(o):
        dev = {"z": z + 1 - 2 * mine}
        if o:
            dev["c"] = 1 - c
        return dev

    def xyat(d, e):
        return {"x": lax.rem(x + (d % 4), 4), "shard": lax.rem(y + (e % 4), 4)}

    def remote(src, dst, ssem, rsem, dev):
        return pltpu.make_async_remote_copy(
            src_ref=src, dst_ref=dst, send_sem=ssem, recv_sem=rsem, device_id=dev, device_id_type=MESH
        )

    barrier = pltpu.get_barrier_semaphore()
    others = [zat(d) for d in (4, 3, 5, 2, 6, 1, 7)]
    others += [xyat(d, e) for d in range(4) for e in range(4) if d or e]
    others += [xcat(d, 1) for d in range(4)] + [partner(1)]
    for dev in others:
        pl.semaphore_signal(barrier, inc=1, device_id=dev, device_id_type=MESH)
    TG[0] = jnp.zeros((8, 128), jnp.int32)
    TG[0, 0:1, 0:PIECE] = tgt_ref[...]

    own_x = pltpu.make_async_copy(x_ref, X.at[0], loc_sem.at[4])
    own_x.start()
    blocks = []
    for p in range(4):
        col = lax.rem(z + (DZ[p] % 8), 8) * 512 + x * 128
        cp = pltpu.make_async_copy(
            table_ref.at[:, pl.ds(pl.multiple_of(col, 128), 128)], TB.at[p], loc_sem.at[p]
        )
        cp.start()
        blocks.append(cp)

    W[0] = w_ref[...].astype(BF16)
    GA[...] = jnp.zeros_like(GA)

    for cp in blocks:
        cp.wait()
    _, lane = iotas((256, 128))
    for q in range(2):
        left = pltpu.roll(TB[2 * q].astype(F32), 64 * c, 1)
        right = pltpu.roll(TB[2 * q + 1].astype(F32), 64 * (1 - c), 1)
        TT[:, q * 128 : q * 128 + 128] = jnp.where(lane < 64, left, right).astype(BF16)

    own_x.wait()
    pl.semaphore_wait(barrier, len(others))

    def target_copy(k, m):
        there = place_of(-KX[k], KC[k], m)
        slot = place_of(0, 0, m)
        return remote(TG.at[slot], TG.at[there], t_s.at[m, k], t_r.at[there], xcat(KX[k], KC[k]))

    others_in_plane = [k for k in range(1, 16) if KM[k] == 0]
    tpair = remote(TG.at[0], TG.at[6], t_s.at[0, 0], t_r.at[6], partner(0))
    tcopies = [[target_copy(k, m) for k in others_in_plane] for m in range(2)]
    tpair.start()
    for tc in tcopies[0]:
        tc.start()

    wcopies = []
    for p in range(1, 4):
        there = block_of(-DZ[p])
        wcopies.append(remote(W.at[0], W.at[there], w_s.at[p], w_r.at[there], zat(DZ[p])))
        wcopies[-1].start()

    lo, hi = pl.ds(0, 160), pl.ds(160, 160)
    xpair = [remote(X.at[0, h], X.at[6, h], z_s.at[i], z_r.at[i], partner(0)) for i, h in enumerate((lo, hi))]

    def around(m):
        own, core, left, right, far = (place_of(d, o, m) for d, o in ((0, 0), (0, 1), (-1, 0), (1, 0), (2, 0)))
        left_core, right_core, far_core = (place_of(d, 1, m) for d in (-1, 1, 2))
        plan = (
            (X.at[own, lo], X.at[left, lo], xcat(1, 0)),
            (X.at[own, hi], X.at[right, hi], xcat(-1, 0)),
            (X.at[own], X.at[core], xcat(0, 1)),
            (X.at[own, hi], X.at[left, hi], xcat(1, 0)),
            (X.at[own, lo], X.at[right, lo], xcat(-1, 0)),
            (X.at[left, lo], X.at[far, lo], xcat(1, 0)),
            (X.at[right, hi], X.at[far, hi], xcat(-1, 0)),
            (X.at[left], X.at[left_core], xcat(0, 1)),
            (X.at[right], X.at[right_core], xcat(0, 1)),
            (X.at[far], X.at[far_core], xcat(0, 1)),
        )
        return [remote(a, b, x_s.at[m, i], x_r.at[m, i], dev) for i, (a, b, dev) in enumerate(plan)]

    xa, xb = around(0), around(1)
    for i in range(5):
        xa[i].start()
    for cp in xpair:
        cp.start()

    tpair.wait_recv()
    for tc in tcopies[1]:
        tc.start()
    for cp in wcopies:
        cp.wait_recv()

    yp, ym, y2 = lax.rem(y + 1, 4), lax.rem(y + 3, 4), lax.rem(y + 2, 4)

    def r1(u, d):
        return remote(S1.at[u, d], R1.at[u, d], y_s.at[0, d, u], y_r.at[0, d, u], yat(1 - 2 * d))

    def r2(u, d):
        return remote(S2.at[u, d], R2.at[u, d], y_s.at[1, d, u], y_r.at[1, d, u], yat(1 - 2 * d))

    def a1(u, d, who):
        ref = E.at[u, who]
        return remote(ref, ref, y_s.at[2, d, u], y_r.at[2, d, u], yat(1 - 2 * d))

    def a2(u, d, who):
        ref = E.at[u, who, :, pl.ds(128 * d, 128)]
        return remote(ref, ref, y_s.at[3, d, u], y_r.at[3, d, u], yat(1 - 2 * d))

    def arrived(u):
        plan = {
            1: ((xa[2], None), (xa[0], xa[5]), (xa[1], xa[6])),
            2: ((xa[3], xa[7]),),
            3: ((xa[4], xa[8]),),
            4: ((xa[7], None), (xpair[0], xb[0], xb[4])),
            5: ((xa[8], None),),
            6: ((xpair[1], xb[1], xb[3], xb[2]),),
            7: ((xb[2], None),),
            8: ((xa[5], None), (xa[6], xa[9])),
            9: ((xa[9], None), (xb[0], xb[5])),
            10: ((xb[3], xb[7]), (xb[1], xb[6])),
            11: ((xb[4], xb[8]),),
            12: ((xb[7], None),),
            13: ((xb[8], None),),
            14: ((xb[5], None), (xb[6], xb[9])),
            15: ((xb[9], None),),
        }
        for turn, steps in plan.items():

            @pl.when(u == turn)
            def _(steps=steps):
                for first, *then in steps:
                    first.wait_recv()
                    for cp in then:
                        if cp is not None:
                            cp.start()

    def forward(u):
        slot = lax.rem(u, 8)
        arrived(u)
        part = lax.dot_general(
            X[u], W[...].reshape(HALF, FEAT), (((1,), (1,)), ((), ())), preferred_element_type=F32
        )
        PF[slot] = part.reshape(4, PIECE, HALF)
        far = PF[slot, y2].astype(BF16)
        S1[u, 0] = far[:, :128]
        S1[u, 1] = far[:, 128:]
        r1(u, 0).start()
        r1(u, 1).start()

        @pl.when(u == 0)
        def _():
            for tc in tcopies[0]:
                tc.wait_recv()

        @pl.when(u == 6)
        def _():
            for tc in tcopies[1]:
                tc.wait_recv()

        row = TG[u][0:1]
        sub, _ = iotas((256, 128))
        one_hot = (sub == row).astype(F32).astype(BF16)
        wanted = lax.dot_general(one_hot, TT[...], (((0,), (0,)), ((), ())), preferred_element_type=F32)
        PF[slot, y] = PF[slot, y] - wanted[:PIECE]

    def reduce_step(u):
        slot = lax.rem(u, 8)
        r1(u, 0).wait_recv()
        r1(u, 1).wait_recv()
        S2[u, 0, :, :128] = (PF[slot, yp, :, :128] + R1[u, 0].astype(F32)).astype(BF16)
        S2[u, 0, :, 128:] = PF[slot, yp, :, 128:].astype(BF16)
        r2(u, 0).start()
        S2[u, 1, :, :128] = PF[slot, ym, :, :128].astype(BF16)
        S2[u, 1, :, 128:] = (PF[slot, ym, :, 128:] + R1[u, 1].astype(F32)).astype(BF16)
        r2(u, 1).start()

    def error_step(u):
        slot = lax.rem(u, 8)
        r2(u, 0).wait_recv()
        r2(u, 1).wait_recv()
        total = PF[slot, y] + R2[u, 0].astype(F32) + R2[u, 1].astype(F32)
        E[u, y] = (total * (1.0 / ROWS)).astype(BF16)
        a1(u, 0, y).start()
        a1(u, 1, y).start()

    def spread_step(u):
        a1(u, 0, ym).wait_recv()
        a2(u, 0, ym).start()
        a1(u, 1, yp).wait_recv()
        a2(u, 1, yp).start()

    def replica(k):
        plane = lax.rem(mine + KM[k], 2)
        return plane * 8 + lax.rem(x + (KX[k] % 4), 4) * 2 + lax.rem(c + KC[k], 2)

    def grad_step(u):
        a2(u, 0, y2).wait_recv()
        a2(u, 1, y2).wait_recv()
        err = E[u].reshape(ROWS, HALF)
        G[u] = lax.dot_general(err, X[u], (((0,), (0,)), ((), ())), preferred_element_type=F32)
        for kk in range(16):

            @pl.when(u == kk)
            def _():
                def block(i, sums):
                    rows = pl.ds(pl.multiple_of(i * 8, 8), 8)
                    sums = list(sums)
                    for j in range(FEAT // 128):
                        cols = pl.ds(j * 128, 128)
                        own = G[kk, rows, cols]
                        for l in range(kk):
                            sums[l] = sums[l] + own * G[l, rows, cols]
                        sums[kk] = sums[kk] + own * own
                    return tuple(sums)

                sums = lax.fori_loop(
                    0, HALF // 8, block, tuple(jnp.zeros((8, 128), F32) for _ in range(kk + 1))
                )
                gram = GA[...]
                for l in range(kk + 1):
                    gram = put_pair(gram, replica(kk), replica(l), sums[l])
                GA[...] = gram

        for d in range(2):
            r1(u, d).wait_send()
            r2(u, d).wait_send()
            a1(u, d, y).wait_send()
            a2(u, d, ym if d == 0 else yp).wait_send()

    def turn(t, carry):
        for n, step in ((3, spread_step), (2, error_step), (1, reduce_step), (0, forward), (4, grad_step)):

            @pl.when((t >= n * LAG) & (t < UNITS + n * LAG))
            def _():
                step(t - n * LAG)

        return carry

    lax.fori_loop(0, UNITS + 4 * LAG, turn, 0)

    def sum_xy(ref, s):
        copies = []
        for i in range(1, 16):
            d, e = i // 4, i % 4
            there = (-d) % 4 * 4 + (-e) % 4
            cp = remote(ref.at[0], ref.at[there], a_s.at[s, i], a_r.at[s, there], xyat(d, e))
            cp.start()
            copies.append(cp)
        for cp in copies:
            cp.wait()
        return jnp.sum(ref[...], axis=0)

    def sum_planes(value):
        AC[0] = value
        near = (xcat(0, 1), partner(0), partner(1))
        copies = [remote(AC.at[0], AC.at[i + 1], a_s.at[3, i], a_r.at[3, i], dev) for i, dev in enumerate(near)]
        for cp in copies:
            cp.start()
        for cp in copies:
            cp.wait()
        AX[0] = jnp.sum(AC[...], axis=0)
        return sum_xy(AX, 0)

    def sum_plane(value):
        BC[0] = value
        cp = remote(BC.at[0], BC.at[1], a_s.at[4, 0], a_r.at[4, 0], xcat(0, 1))
        cp.start()
        cp.wait()
        BX[0] = BC[0] + BC[1]
        return sum_xy(BX, 1)

    def sum_z(value):
        AZ[0] = value
        copies = []
        for d in range(1, 8):
            cp = remote(AZ.at[0], AZ.at[8 - d], a_s.at[2, d], a_r.at[2, 8 - d], zat(d))
            cp.start()
            copies.append(cp)
        for cp in copies:
            cp.wait()
        return functools.reduce(jnp.add, [AZ[k] for k in range(8)])

    coef = tree_coefficients(sum_planes(GA[...]), (1, 2, 4, 8))
    weights = [pick(coef, replica(k)) for k in range(16)]

    ccopies = {}
    for p in (3, 1, 2, 0):

        def mix(i, carry):
            rows = pl.ds(pl.multiple_of(p * 64 + i * 16, 16), 16)
            total = weights[0] * G[0, rows, :]
            for k in range(1, 16):
                total = total + weights[k] * G[k, rows, :]
            here = pl.ds(pl.multiple_of(i * 16, 16), 16)
            if p == 0:
                OWN[here, :] = total
            else:
                CS[p, here, :] = total.astype(BF16)
            return carry

        lax.fori_loop(0, 4, mix, 0)
        if p:
            there = block_of(-DZ[p])
            ccopies[there] = remote(CS.at[p], CB.at[there], c_s.at[p], c_r.at[there], zat(DZ[p]))
            ccopies[there].start()

    def pair(p):
        return lax.rem(z + (DZ[p] % 8), 8) // 2

    gram = jnp.zeros((8, 128), F32)
    for p in range(4):
        if p:
            ccopies[p].wait_recv()

        def block(i, sums, p=p):
            rows = pl.ds(pl.multiple_of(i * 16, 16), 16)
            sums = list(sums)
            for j in range(FEAT // 128):
                cols = pl.ds(j * 128, 128)

                def read(q):
                    return CB[q, rows, cols].astype(F32) if q else OWN[rows, cols]

                own = read(p)
                for l in range(p + 1):
                    prod = own * read(l)
                    sums[l] = sums[l] + prod[:8] + prod[8:]
            return tuple(sums)

        sums = lax.fori_loop(0, 4, block, tuple(jnp.zeros((8, 128), F32) for _ in range(p + 1)))
        for l in range(p + 1):
            gram = put_pair(gram, pair(p), pair(l), sums[l])

    coef = tree_coefficients(sum_z(sum_plane(gram)), (1, 2))
    weights = [pick(coef, pair(p)) for p in range(4)]

    def final(i, carry):
        rows = pl.ds(pl.multiple_of(i * 16, 16), 16)
        near = weights[0] * OWN[rows, :] + weights[1] * CB[1, rows, :].astype(F32)
        far = weights[2] * CB[2, rows, :].astype(F32) + weights[3] * CB[3, rows, :].astype(F32)
        near_ref[rows, :] = near
        far_ref[rows, :] = far
        return carry

    lax.fori_loop(0, 4, final, 0)

    for cp in wcopies + xa + xb + xpair + [tpair] + tcopies[0] + tcopies[1] + list(ccopies.values()):
        cp.wait_send()


def on_device(inputs, weight, table, targets):
    vmem = pl.BlockSpec(memory_space=pltpu.VMEM)
    anywhere = pl.BlockSpec(memory_space=pl.ANY)
    dma = pltpu.SemaphoreType.DMA
    near, far = pl.pallas_call(
        kernel,
        out_shape=[jax.ShapeDtypeStruct((64, FEAT), F32)] * 2,
        in_specs=[anywhere, vmem, vmem, anywhere],
        out_specs=[vmem] * 2,
        scratch_shapes=[
            pltpu.VMEM((16, ROWS, FEAT), BF16),
            pltpu.VMEM((4, 64, FEAT), BF16),
            pltpu.VMEM((16, 8, 128), jnp.int32),
            pltpu.VMEM((4, 256, 128), BF16),
            pltpu.VMEM((256, HALF), BF16),
            pltpu.VMEM((8, 4, PIECE, HALF), F32),
            pltpu.VMEM((UNITS, 2, PIECE, 128), BF16),
            pltpu.VMEM((UNITS, 2, PIECE, HALF), BF16),
            pltpu.VMEM((UNITS, 2, PIECE, 128), BF16),
            pltpu.VMEM((UNITS, 2, PIECE, HALF), BF16),
            pltpu.VMEM((16, 4, PIECE, HALF), BF16),
            pltpu.VMEM((16, HALF, FEAT), F32),
            pltpu.VMEM((16, 128), F32),
            pltpu.VMEM((4, 64, FEAT), BF16),
            pltpu.VMEM((4, 64, FEAT), BF16),
            pltpu.VMEM((64, FEAT), F32),
            pltpu.VMEM((4, 16, 128), F32),
            pltpu.VMEM((16, 16, 128), F32),
            pltpu.VMEM((2, 8, 128), F32),
            pltpu.VMEM((16, 8, 128), F32),
            pltpu.VMEM((8, 8, 128), F32),
            dma((5,)),
            dma((4,)),
            dma((4,)),
            dma((2,)),
            dma((2,)),
            dma((2, 10)),
            dma((2, 10)),
            dma((2, 16)),
            dma((16,)),
            dma((4, 2, UNITS)),
            dma((4, 2, UNITS)),
            dma((4,)),
            dma((4,)),
            dma((5, 16)),
            dma((5, 16)),
        ],
        compiler_params=pltpu.CompilerParams(
            collective_id=0, has_side_effects=True, vmem_limit_bytes=56 * 1024 * 1024
        ),
    )(inputs, weight.T, targets[None], table)
    combined = near + far
    return combined.T, (weight.T - STEP * combined).T


def solution(mesh):
    split = Mesh(mesh.devices.reshape(8, 4, 2, mesh.shape["shard"]), AXES)
    return jax.shard_map(
        on_device,
        mesh=split,
        in_specs=(P(REP, "shard"), P("shard", REP), P(), P(REP + ("shard",))),
        out_specs=(P("shard", REP), P("shard", REP)),
        check_vma=False,
    )
```

time: 127 us -> 123 us (0.969)
  Pallas kernels: 124 us -> 120 us
    pallas_call x1, Pallas kernels: 124 us -> 120 us  [on_device(): pl.pallas_call(kernel, out_shape=[jax.ShapeDtypeStruct((64, FEAT), F32)]...]
where the time goes in v5:
time: 123 us
  Pallas kernels  120 us (98%)
  other arithmetic  1.88 us (2%)
    pallas_call x1, Pallas kernels, on_device(): pl.pallas_call(kernel, out_shape=[jax.ShapeDtypeStruct((64, FEAT), F32)]...  120 us

profile of v5, /device:TPU:1, one launch (start us, length us, event | category | flops | bytes accessed | tf_op | source)
XLA Modules:
  0.0 122.8 jit_solution(12139905507041035736)
XLA Ops:
  0.6 0.0 copy-start
  0.6 120.2 %shard_map.59 = (f32[64,1024]{1,0:T(8,128)}, f32[64,1024]{1,0:T(8,128)}) custom-call(bf16[320,1024]{1,0:T(8,128)(2,1)} %x_ref.1, f32[64,1024]{1,0:T(8,128)} %bitcast.7, s32[1,80]{1,0:T(1,128)} %bitcast.8, bf16[256,4096]{1,0:T(8,128)(2,1)} %table_ref.1), custom_call_target="tpu_custom_call" | custom-call | tf_op jit(solution)/shard_map/pallas_call | solution.py:461
  120.9 0.0 copy-done
  120.9 1.9 %subtract_bitcast_fusion = (f32[1024,64]{0,1:T(8,128)}, f32[1024,64]{0,1:T(8,128)}) fusion(f32[64,1024]{1,0:T(8,128)} %get-tuple-element.4, f32[64,1024]{1,0:T(8,128)} %get-tuple-element.5, f32[1024,64]{0,1:T(8,128)S(1)} %copy-done), kind=kLoop, calls=%fused_computation | loop fusion | flops 196608 | bytes 1310720 | tf_op jit(solution)/shard_map/transpose | solution.py:509
Async XLA Ops:
  0.6 120.3 %copy-start = (f32[1024,64]{0,1:T(8,128)S(1)}, f32[1024,64]{0,1:T(8,128)}, u32[]{:S(2)}) copy-start(f32[1024,64]{0,1:T(8,128)} %param.5) | copy-start | bytes 786436

commit v6 on v5

--- a/solution.py
+++ b/solution.py
@@ -22,7 +22,7 @@
 DZ = (0, 2, -2, 4)
 
 ROWS, FEAT, PIECE, HALF = 320, 1024, 80, 256
-UNITS, LAG = 16, 2
+UNITS, LAST = 16, 14
 
 
 def place_of(steps, other, plane):
@@ -74,10 +74,20 @@
     return jnp.where(((sub == i) & (lane == j)) | ((sub == j) & (lane == i)), v, gram)
 
 
+def put_line(gram, i, others, products):
+    sub, lane = iotas(gram.shape)
+    lines = jnp.zeros(gram.shape, F32)
+    for j, part in zip(others, products):
+        lines = jnp.where(sub == j, jnp.sum(part, axis=0, keepdims=True), lines)
+    column = jnp.sum(lines, axis=1, keepdims=True)
+    row = jnp.sum(jnp.where(sub == lane, column, 0.0), axis=0, keepdims=True)
+    return jnp.where(lane == i, column, jnp.where(sub == i, row, gram))
+
+
 def kernel(
     x_ref, w_ref, tgt_ref, table_ref, near_ref, far_ref,
     X, W, TG, TB, TT, PF, S1, S2, R1, R2, E, G, GA, CS, CB, OWN, AC, AX, BC, BX, AZ,
-    loc_sem, w_s, w_r, z_s, z_r, x_s, x_r, t_s, t_r, y_s, y_r, c_s, c_r, a_s, a_r,
+    loc_sem, w_s, w_r, z_s, z_r, x_s, x_r, t_s, t_r, y_s, y_r, d_s, d_r, c_s, c_r, a_s, a_r,
 ):
     z, x = lax.axis_index("z"), lax.axis_index("x")
     c, y = lax.axis_index("c"), lax.axis_index("shard")
@@ -158,11 +168,16 @@
     for tc in tcopies[0]:
         tc.start()
 
-    wcopies = []
-    for p in range(1, 4):
-        there = block_of(-DZ[p])
-        wcopies.append(remote(W.at[0], W.at[there], w_s.at[p], w_r.at[there], zat(DZ[p])))
-        wcopies[-1].start()
+    upper, lower = pl.ds(0, 32), pl.ds(32, 32)
+    plan = (
+        (W.at[0], W.at[2], 2),
+        (W.at[0], W.at[1], -2),
+        (W.at[2, upper], W.at[3, upper], 2),
+        (W.at[1, lower], W.at[3, lower], -2),
+    )
+    wcopies = [remote(a, b, w_s.at[i], w_r.at[i], zat(d)) for i, (a, b, d) in enumerate(plan)]
+    wcopies[0].start()
+    wcopies[1].start()
 
     lo, hi = pl.ds(0, 160), pl.ds(160, 160)
     xpair = [remote(X.at[0, h], X.at[6, h], z_s.at[i], z_r.at[i], partner(0)) for i, h in enumerate((lo, hi))]
@@ -176,8 +191,8 @@
             (X.at[own], X.at[core], xcat(0, 1)),
             (X.at[own, hi], X.at[left, hi], xcat(1, 0)),
             (X.at[own, lo], X.at[right, lo], xcat(-1, 0)),
-            (X.at[left, lo], X.at[far, lo], xcat(1, 0)),
-            (X.at[right, hi], X.at[far, hi], xcat(-1, 0)),
+            (X.at[left, lo], X.at[far, lo], xcat(1, 0)) if m == 0 else (X.at[8, lo], X.at[far, lo], partner(0)),
+            (X.at[right, hi], X.at[far, hi], xcat(-1, 0)) if m == 0 else (X.at[8, hi], X.at[far, hi], partner(0)),
             (X.at[left], X.at[left_core], xcat(0, 1)),
             (X.at[right], X.at[right_core], xcat(0, 1)),
             (X.at[far], X.at[far_core], xcat(0, 1)),
@@ -187,14 +202,17 @@
     xa, xb = around(0), around(1)
     for i in range(5):
         xa[i].start()
+
+    for i in (0, 1):
+        wcopies[i].wait_recv()
+        wcopies[i + 2].start()
     for cp in xpair:
         cp.start()
-
     tpair.wait_recv()
     for tc in tcopies[1]:
         tc.start()
-    for cp in wcopies:
-        cp.wait_recv()
+    for i in (2, 3):
+        wcopies[i].wait_recv()
 
     yp, ym, y2 = lax.rem(y + 1, 4), lax.rem(y + 3, 4), lax.rem(y + 2, 4)
 
@@ -207,6 +225,10 @@
     def a1(u, d, who):
         ref = E.at[u, who]
         return remote(ref, ref, y_s.at[2, d, u], y_r.at[2, d, u], yat(1 - 2 * d))
+
+    def a3(u, who):
+        ref = E.at[u, who]
+        return remote(ref, ref, d_s.at[u - LAST], d_r.at[u - LAST], yat(2))
 
     def a2(u, d, who):
         ref = E.at[u, who, :, pl.ds(128 * d, 128)]
@@ -218,13 +240,12 @@
             2: ((xa[3], xa[7]),),
             3: ((xa[4], xa[8]),),
             4: ((xa[7], None), (xpair[0], xb[0], xb[4])),
-            5: ((xa[8], None),),
-            6: ((xpair[1], xb[1], xb[3], xb[2]),),
+            5: ((xa[8], None), (xpair[1], xb[1], xb[3], xb[2])),
+            6: ((xa[5], xb[5]), (xa[6], xb[6], xa[9])),
             7: ((xb[2], None),),
-            8: ((xa[5], None), (xa[6], xa[9])),
-            9: ((xa[9], None), (xb[0], xb[5])),
-            10: ((xb[3], xb[7]), (xb[1], xb[6])),
-            11: ((xb[4], xb[8]),),
+            9: ((xa[9], None),),
+            10: ((xb[0], None), (xb[3], xb[7])),
+            11: ((xb[1], None), (xb[4], xb[8])),
             12: ((xb[7], None),),
             13: ((xb[8], None),),
             14: ((xb[5], None), (xb[6], xb[9])),
@@ -241,7 +262,7 @@
                             cp.start()
 
     def forward(u):
-        slot = lax.rem(u, 8)
+        slot = u % 8
         arrived(u)
         part = lax.dot_general(
             X[u], W[...].reshape(HALF, FEAT), (((1,), (1,)), ((), ())), preferred_element_type=F32
@@ -270,7 +291,7 @@
         PF[slot, y] = PF[slot, y] - wanted[:PIECE]
 
     def reduce_step(u):
-        slot = lax.rem(u, 8)
+        slot = u % 8
         r1(u, 0).wait_recv()
         r1(u, 1).wait_recv()
         S2[u, 0, :, :128] = (PF[slot, yp, :, :128] + R1[u, 0].astype(F32)).astype(BF16)
@@ -281,7 +302,7 @@
         r2(u, 1).start()
 
     def error_step(u):
-        slot = lax.rem(u, 8)
+        slot = u % 8
         r2(u, 0).wait_recv()
         r2(u, 1).wait_recv()
         total = PF[slot, y] + R2[u, 0].astype(F32) + R2[u, 1].astype(F32)
@@ -289,6 +310,10 @@
         a1(u, 0, y).start()
         a1(u, 1, y).start()
 
+        @pl.when(u >= LAST)
+        def _():
+            a3(u, y).start()
+
     def spread_step(u):
         a1(u, 0, ym).wait_recv()
         a2(u, 0, ym).start()
@@ -300,8 +325,18 @@
         return plane * 8 + lax.rem(x + (KX[k] % 4), 4) * 2 + lax.rem(c + KC[k], 2)
 
     def grad_step(u):
-        a2(u, 0, y2).wait_recv()
-        a2(u, 1, y2).wait_recv()
+
+        @pl.when(u < LAST)
+        def _():
+            a2(u, 0, y2).wait_recv()
+            a2(u, 1, y2).wait_recv()
+
+        @pl.when(u >= LAST)
+        def _():
+            a1(u, 0, ym).wait_recv()
+            a1(u, 1, yp).wait_recv()
+            a3(u, y2).wait_recv()
+
         err = E[u].reshape(ROWS, HALF)
         G[u] = lax.dot_general(err, X[u], (((0,), (0,)), ((), ())), preferred_element_type=F32)
         for kk in range(16):
@@ -322,27 +357,40 @@
                 sums = lax.fori_loop(
                     0, HALF // 8, block, tuple(jnp.zeros((8, 128), F32) for _ in range(kk + 1))
                 )
-                gram = GA[...]
-                for l in range(kk + 1):
-                    gram = put_pair(gram, replica(kk), replica(l), sums[l])
-                GA[...] = gram
+                GA[...] = put_line(GA[...], replica(kk), [replica(l) for l in range(kk + 1)], sums)
 
         for d in range(2):
-            r1(u, d).wait_send()
             r2(u, d).wait_send()
             a1(u, d, y).wait_send()
-            a2(u, d, ym if d == 0 else yp).wait_send()
+            r1(u, d).wait_send()
+
+        @pl.when(u < LAST)
+        def _():
+            a2(u, 0, ym).wait_send()
+            a2(u, 1, yp).wait_send()
+
+        @pl.when(u >= LAST)
+        def _():
+            a3(u, y).wait_send()
 
     def turn(t, carry):
-        for n, step in ((3, spread_step), (2, error_step), (1, reduce_step), (0, forward), (4, grad_step)):
-
-            @pl.when((t >= n * LAG) & (t < UNITS + n * LAG))
+        def at(u, low, high, step):
+            @pl.when((u >= low) & (u < high))
             def _():
-                step(t - n * LAG)
-
+                step(u)
+
+        at(t - 6, 0, LAST, spread_step)
+        at(t - 4, 0, UNITS, error_step)
+        at(t - 2, 0, UNITS, reduce_step)
+
+        @pl.when(t < UNITS)
+        def _():
+            forward(t)
+
+        at(t - 8, 0, UNITS, grad_step)
         return carry
 
-    lax.fori_loop(0, UNITS + 4 * LAG, turn, 0)
+    lax.fori_loop(0, UNITS + 8, turn, 0)
 
     def sum_xy(ref, s):
         copies = []
@@ -410,6 +458,9 @@
             ccopies[there] = remote(CS.at[p], CB.at[there], c_s.at[p], c_r.at[there], zat(DZ[p]))
             ccopies[there].start()
 
+    for cp in wcopies + xa + xb + xpair + [tpair] + tcopies[0] + tcopies[1]:
+        cp.wait_send()
+
     def pair(p):
         return lax.rem(z + (DZ[p] % 8), 8) // 2
 
@@ -450,7 +501,7 @@
 
     lax.fori_loop(0, 4, final, 0)
 
-    for cp in wcopies + xa + xb + xpair + [tpair] + tcopies[0] + tcopies[1] + list(ccopies.values()):
+    for cp in ccopies.values():
         cp.wait_send()
 
 
@@ -496,6 +547,8 @@
             dma((16,)),
             dma((4, 2, UNITS)),
             dma((4, 2, UNITS)),
+            dma((UNITS - LAST,)),
+            dma((UNITS - LAST,)),
             dma((4,)),
             dma((4,)),
             dma((5, 16)),

time: 123 us -> 122 us (level)
  no operation moved by 1% of the time
where the time goes in v6:
time: 122 us
  Pallas kernels  119 us (98%)
  other arithmetic  1.88 us (2%)
    pallas_call x1, Pallas kernels, on_device(): pl.pallas_call(kernel, out_shape=[jax.ShapeDtypeStruct((64, FEAT), F32)]...  119 us

profile of v6, /device:TPU:1, one launch (start us, length us, event | category | flops | bytes accessed | tf_op | source)
XLA Modules:
  0.0 121.6 jit_solution(18166110073318687869)
XLA Ops:
  0.6 0.0 copy-start
  0.6 119.0 %shard_map.59 = (f32[64,1024]{1,0:T(8,128)}, f32[64,1024]{1,0:T(8,128)}) custom-call(bf16[320,1024]{1,0:T(8,128)(2,1)} %x_ref.1, f32[64,1024]{1,0:T(8,128)} %bitcast.7, s32[1,80]{1,0:T(1,128)} %bitcast.8, bf16[256,4096]{1,0:T(8,128)(2,1)} %table_ref.1), custom_call_target="tpu_custom_call" | custom-call | tf_op jit(solution)/shard_map/pallas_call | solution.py:512
  119.7 0.0 copy-done
  119.7 1.9 %subtract_bitcast_fusion = (f32[1024,64]{0,1:T(8,128)}, f32[1024,64]{0,1:T(8,128)}) fusion(f32[64,1024]{1,0:T(8,128)} %get-tuple-element.4, f32[64,1024]{1,0:T(8,128)} %get-tuple-element.5, f32[1024,64]{0,1:T(8,128)S(1)} %copy-done), kind=kLoop, calls=%fused_computation | loop fusion | flops 196608 | bytes 1310720 | tf_op jit(solution)/shard_map/transpose | solution.py:562
Async XLA Ops:
  0.6 119.0 %copy-start = (f32[1024,64]{0,1:T(8,128)S(1)}, f32[1024,64]{0,1:T(8,128)}, u32[]{:S(2)}) copy-start(f32[1024,64]{0,1:T(8,128)} %param.5) | copy-start | bytes 786436

commit v7 on v6

--- a/solution.py
+++ b/solution.py
@@ -22,7 +22,7 @@
 DZ = (0, 2, -2, 4)
 
 ROWS, FEAT, PIECE, HALF = 320, 1024, 80, 256
-UNITS, LAST = 16, 14
+UNITS, LAST = 16, 15
 
 
 def place_of(steps, other, plane):
@@ -239,10 +239,10 @@
             1: ((xa[2], None), (xa[0], xa[5]), (xa[1], xa[6])),
             2: ((xa[3], xa[7]),),
             3: ((xa[4], xa[8]),),
-            4: ((xa[7], None), (xpair[0], xb[0], xb[4])),
-            5: ((xa[8], None), (xpair[1], xb[1], xb[3], xb[2])),
-            6: ((xa[5], xb[5]), (xa[6], xb[6], xa[9])),
-            7: ((xb[2], None),),
+            4: ((xa[7], None),),
+            5: ((xa[8], None), (xpair[0], xb[0], xb[4]),),
+            6: ((xpair[1], xb[1], xb[3], xb[2]),),
+            7: ((xb[2], None), (xa[5], xb[5]), (xa[6], xb[6], xa[9]),),
             9: ((xa[9], None),),
             10: ((xb[0], None), (xb[3], xb[7])),
             11: ((xb[1], None), (xb[4], xb[8])),
@@ -382,12 +382,11 @@
         at(t - 6, 0, LAST, spread_step)
         at(t - 4, 0, UNITS, error_step)
         at(t - 2, 0, UNITS, reduce_step)
-
+        at(t - 8, 0, UNITS, grad_step)
         @pl.when(t < UNITS)
         def _():
             forward(t)
 
-        at(t - 8, 0, UNITS, grad_step)
         return carry
 
     lax.fori_loop(0, UNITS + 8, turn, 0)

time: 122 us -> 121 us (level)
  no operation moved by 1% of the time
where the time goes in v7:
time: 121 us
  Pallas kernels  118 us (98%)
  other arithmetic  1.88 us (2%)
    pallas_call x1, Pallas kernels, on_device(): pl.pallas_call(kernel, out_shape=[jax.ShapeDtypeStruct((64, FEAT), F32)]...  118 us

profile of v7, /device:TPU:1, one launch (start us, length us, event | category | flops | bytes accessed | tf_op | source)
XLA Modules:
  0.0 120.9 jit_solution(4250170708577617961)
XLA Ops:
  0.6 0.0 copy-start
  0.6 118.3 %shard_map.59 = (f32[64,1024]{1,0:T(8,128)}, f32[64,1024]{1,0:T(8,128)}) custom-call(bf16[320,1024]{1,0:T(8,128)(2,1)} %x_ref.1, f32[64,1024]{1,0:T(8,128)} %bitcast.7, s32[1,80]{1,0:T(1,128)} %bitcast.8, bf16[256,4096]{1,0:T(8,128)(2,1)} %table_ref.1), custom_call_target="tpu_custom_call" | custom-call | tf_op jit(solution)/shard_map/pallas_call | solution.py:511
  119.0 0.0 copy-done
  119.0 1.9 %subtract_bitcast_fusion = (f32[1024,64]{0,1:T(8,128)}, f32[1024,64]{0,1:T(8,128)}) fusion(f32[64,1024]{1,0:T(8,128)} %get-tuple-element.4, f32[64,1024]{1,0:T(8,128)} %get-tuple-element.5, f32[1024,64]{0,1:T(8,128)S(1)} %copy-done), kind=kLoop, calls=%fused_computation | loop fusion | flops 196608 | bytes 1310720 | tf_op jit(solution)/shard_map/transpose | solution.py:561
Async XLA Ops:
  0.6 118.3 %copy-start = (f32[1024,64]{0,1:T(8,128)S(1)}, f32[1024,64]{0,1:T(8,128)}, u32[]{:S(2)}) copy-start(f32[1024,64]{0,1:T(8,128)} %param.5) | copy-start | bytes 786436

commit v8 on v7

--- a/solution.py
+++ b/solution.py
@@ -393,7 +393,7 @@
 
     def sum_xy(ref, s):
         copies = []
-        for i in range(1, 16):
+        for i in (10, 6, 14, 9, 11, 2, 8, 5, 7, 13, 15, 1, 3, 4, 12):
             d, e = i // 4, i % 4
             there = (-d) % 4 * 4 + (-e) % 4
             cp = remote(ref.at[0], ref.at[there], a_s.at[s, i], a_r.at[s, there], xyat(d, e))
@@ -425,7 +425,7 @@
     def sum_z(value):
         AZ[0] = value
         copies = []
-        for d in range(1, 8):
+        for d in (4, 3, 5, 2, 6, 1, 7):
             cp = remote(AZ.at[0], AZ.at[8 - d], a_s.at[2, d], a_r.at[2, 8 - d], zat(d))
             cp.start()
             copies.append(cp)

time: 121 us -> 120 us (level)
  no operation moved by 1% of the time
where the time goes in v8:
time: 120 us
  Pallas kernels  118 us (98%)
  other arithmetic  1.88 us (2%)
    pallas_call x1, Pallas kernels, on_device(): pl.pallas_call(kernel, out_shape=[jax.ShapeDtypeStruct((64, FEAT), F32)]...  118 us

profile of v8, /device:TPU:1, one launch (start us, length us, event | category | flops | bytes accessed | tf_op | source)
XLA Modules:
  0.0 120.1 jit_solution(4180732719181575628)
XLA Ops:
  0.6 0.0 copy-start
  0.6 117.6 %shard_map.59 = (f32[64,1024]{1,0:T(8,128)}, f32[64,1024]{1,0:T(8,128)}) custom-call(bf16[320,1024]{1,0:T(8,128)(2,1)} %x_ref.1, f32[64,1024]{1,0:T(8,128)} %bitcast.7, s32[1,80]{1,0:T(1,128)} %bitcast.8, bf16[256,4096]{1,0:T(8,128)(2,1)} %table_ref.1), custom_call_target="tpu_custom_call" | custom-call | tf_op jit(solution)/shard_map/pallas_call | solution.py:511
  118.2 0.0 copy-done
  118.2 1.9 %subtract_bitcast_fusion = (f32[1024,64]{0,1:T(8,128)}, f32[1024,64]{0,1:T(8,128)}) fusion(f32[64,1024]{1,0:T(8,128)} %get-tuple-element.4, f32[64,1024]{1,0:T(8,128)} %get-tuple-element.5, f32[1024,64]{0,1:T(8,128)S(1)} %copy-done), kind=kLoop, calls=%fused_computation | loop fusion | flops 196608 | bytes 1310720 | tf_op jit(solution)/shard_map/transpose | solution.py:561
Async XLA Ops:
  0.6 117.6 %copy-start = (f32[1024,64]{0,1:T(8,128)S(1)}, f32[1024,64]{0,1:T(8,128)}, u32[]{:S(2)}) copy-start(f32[1024,64]{0,1:T(8,128)} %param.5) | copy-start | bytes 786436
